TPU v7x, 512 devices: a whole 4x4x16 slice. The times are simulated.
512 devices in a mesh: dp: 32 (over y, x, core), seq: 16 (over z).
Axes of the slice: x: 4, y: 4, z: 16, core: 2. Of those that a mesh axis runs over, the one named last changes fastest.
Arguments:
- big_qkv: bfloat16 [32768, 3840], P(('dp', 'seq')), may hold values from -6 to 6
- big_grad: bfloat16 [32768, 1280], P(('dp', 'seq')), may hold values from -18 to 18
- small_qkv: bfloat16 [65536, 3840], P(('dp', 'seq')), may hold values from -6 to 6
- small_grad: bfloat16 [65536, 1280], P(('dp', 'seq')), may hold values from -18 to 18
- small_ids: int32 [512, 128], P(('dp', 'seq')), may hold values from 0 to 1, as said below
Outputs:
- big_dqkv: bfloat16 [32768, 3840], P(('dp', 'seq'))
- small_dqkv: bfloat16 [65536, 3840], P(('dp', 'seq'))
- query_bias_grad: float32 [1280], replicated
Inputs may be any that keep to these rules, and one draw needn't show every extreme that they name: `small_ids`: the rows of one device form one image of 128 patches (all 0), or two images of 64 patches each (0 then 1).
All inputs are finite; a program needn't handle non-finite values.
Results may differ from a plain program's by a relative error of at most 0.0067.
Values may be sent and summed in bfloat16 or wider, within the bound.
No kernel may reach another device: no remote copies, remote signals or barrier semaphores. Data moves between devices by JAX's collectives and lax.ppermute only.
A program may use at most 128 MiB of HBM per device.

v0:
```python
import jax
import jax.numpy as jnp
from jax import lax
from jax.sharding import PartitionSpec as P

HEAD = 80


def split_heads(packed):
    return (packed[..., :HEAD], packed[..., HEAD : 2 * HEAD], packed[..., 2 * HEAD :])


def score_rows(query_rows, key_rows, allowed):
    scores = jnp.einsum(
        "hqd,hkd->hqk", query_rows, key_rows, preferred_element_type=jnp.float32
    ) * HEAD ** (-0.5)
    scores = jnp.where(allowed, scores, -1e30)
    return scores


def small_group(packed, grad_rows, allowed):
    query_rows, key_rows, value_rows = split_heads(packed)
    scores = score_rows(query_rows, key_rows, allowed)
    row_top = jnp.max(scores, axis=-1, keepdims=True)
    exponent = jnp.exp(scores - row_top)
    attention = exponent / jnp.sum(exponent, axis=-1, keepdims=True)
    weights = attention.astype(jnp.bfloat16)
    attended = jnp.einsum("hqk,hkd->hqd", weights, value_rows, preferred_element_type=jnp.float32)
    row_delta = jnp.sum(grad_rows.astype(jnp.float32) * attended, axis=-1, keepdims=True)
    upstream = jnp.einsum("hqd,hkd->hqk", grad_rows, value_rows, preferred_element_type=jnp.float32)
    slopes = (attention * (upstream - row_delta)).astype(jnp.bfloat16)
    query_grad = (
        jnp.einsum("hqk,hkd->hqd", slopes, key_rows, preferred_element_type=jnp.float32)
        * HEAD ** (-0.5)
    ).astype(jnp.bfloat16)
    key_grad = (
        jnp.einsum("hqk,hqd->hkd", slopes, query_rows, preferred_element_type=jnp.float32)
        * HEAD ** (-0.5)
    ).astype(jnp.bfloat16)
    value_grad = jnp.einsum(
        "hqk,hqd->hkd", weights, grad_rows, preferred_element_type=jnp.float32
    ).astype(jnp.bfloat16)
    return jnp.concatenate([query_grad, key_grad, value_grad], axis=-1)


def query_total(gradients, head_count):
    total_rows = gradients.shape[0]
    picked = gradients.reshape(total_rows, head_count, 3 * HEAD)[:, :, :HEAD].astype(jnp.float32)
    return jnp.sum(picked, axis=0).reshape(head_count * HEAD)


def local(big_qkv, big_grad, small_qkv, small_grad, small_ids):
    rows_dev = big_qkv.shape[0]
    head_count = big_grad.shape[1] // HEAD
    packed = big_qkv.reshape(rows_dev, head_count, 3 * HEAD)
    grads = big_grad.reshape(rows_dev, head_count, HEAD)
    query_own = packed[..., :HEAD]
    key_own = packed[..., HEAD : 2 * HEAD]
    value_own = packed[..., 2 * HEAD :]
    whole = lax.all_gather(packed[..., HEAD:], "seq", axis=0, tiled=True)
    group_size = 4
    query_parts = []
    tops = []
    totals = []
    deltas = []
    for group in range(head_count // group_size):
        lower = group * group_size
        upper = lower + group_size
        query_part = query_own[:, lower:upper]
        grad_part = grads[:, lower:upper]
        key_part = whole[:, lower:upper, :HEAD]
        value_part = whole[:, lower:upper, HEAD:]
        scores = jnp.einsum(
            "qhd,khd->hqk", query_part, key_part, preferred_element_type=jnp.float32
        ) * HEAD ** (-0.5)
        row_top = jnp.max(scores, axis=-1)
        exponent = jnp.exp(scores - row_top[..., None])
        row_total = jnp.sum(exponent, axis=-1)
        attention = exponent / row_total[..., None]
        weights = attention.astype(jnp.bfloat16)
        attended = jnp.einsum(
            "hqk,khd->qhd", weights, value_part, preferred_element_type=jnp.float32
        )
        row_delta = jnp.transpose(
            jnp.sum(grad_part.astype(jnp.float32) * attended, axis=-1), (1, 0)
        )
        upstream = jnp.einsum(
            "qhd,khd->hqk", grad_part, value_part, preferred_element_type=jnp.float32
        )
        slopes = (attention * (upstream - row_delta[..., None])).astype(jnp.bfloat16)
        query_grad = (
            jnp.einsum("hqk,khd->qhd", slopes, key_part, preferred_element_type=jnp.float32)
            * HEAD ** (-0.5)
        ).astype(jnp.bfloat16)
        query_parts.append(query_grad)
        tops.append(row_top)
        totals.append(row_total)
        deltas.append(row_delta)
    query_grad = jnp.concatenate(query_parts, axis=1)
    stats = (
        lax.all_gather(jnp.concatenate(tops, axis=0), "seq", axis=1, tiled=True),
        lax.all_gather(jnp.concatenate(totals, axis=0), "seq", axis=1, tiled=True),
        lax.all_gather(jnp.concatenate(deltas, axis=0), "seq", axis=1, tiled=True),
    )
    query_piece = lax.all_gather(query_own, "seq", axis=0, tiled=True)
    grad_piece = lax.all_gather(grads, "seq", axis=0, tiled=True)
    key_terms = []
    value_terms = []
    for group in range(head_count // group_size):
        lower = group * group_size
        upper = lower + group_size
        top_part = stats[0][lower:upper]
        total_part = stats[1][lower:upper]
        delta_part = stats[2][lower:upper]
        query_part = query_piece[:, lower:upper]
        grad_part = grad_piece[:, lower:upper]
        scores = jnp.einsum(
            "qhd,khd->hqk", query_part, key_own[:, lower:upper], preferred_element_type=jnp.float32
        ) * HEAD ** (-0.5)
        attention = jnp.exp(scores - top_part[..., None]) / total_part[..., None]
        weights = attention.astype(jnp.bfloat16)
        upstream = jnp.einsum(
            "qhd,khd->hqk", grad_part, value_own[:, lower:upper], preferred_element_type=jnp.float32
        )
        slopes = (attention * (upstream - delta_part[..., None])).astype(jnp.bfloat16)
        key_terms.append(
            jnp.einsum("hqk,qhd->khd", slopes, query_part, preferred_element_type=jnp.float32)
        )
        value_terms.append(
            jnp.einsum("hqk,qhd->khd", weights, grad_part, preferred_element_type=jnp.float32)
        )
    key_sum = jnp.concatenate(key_terms, axis=1)
    value_sum = jnp.concatenate(value_terms, axis=1)
    key_grad = (key_sum * HEAD ** (-0.5)).astype(jnp.bfloat16)
    value_grad = value_sum.astype(jnp.bfloat16)
    big_out = jnp.concatenate([query_grad, key_grad, value_grad], axis=-1).reshape(
        rows_dev, 3 * head_count * HEAD
    )
    small_rows = small_qkv.shape[0]
    group_size = 4
    small_heads = jnp.transpose(small_qkv.reshape(small_rows, head_count, 3 * HEAD), (1, 0, 2))
    small_grad_heads = jnp.transpose(small_grad.reshape(small_rows, head_count, HEAD), (1, 0, 2))
    small_heads = small_heads.reshape(head_count // group_size, group_size, small_rows, 3 * HEAD)
    small_grad_heads = small_grad_heads.reshape(
        head_count // group_size, group_size, small_rows, HEAD
    )
    labels = small_ids[0]
    allowed = labels[:, None] == labels[None, :]
    small_result = lax.map(
        lambda couple: small_group(couple[0], couple[1], allowed), (small_heads, small_grad_heads)
    )
    small_result = small_result.reshape(head_count, small_rows, 3 * HEAD)
    small_out = jnp.transpose(small_result, (1, 0, 2)).reshape(small_rows, 3 * head_count * HEAD)
    local_sum = query_total(big_out, head_count) + query_total(small_out, head_count)
    bias_grad = lax.psum(local_sum, ("dp", "seq"))
    return (big_out, small_out, bias_grad)


def solution(mesh):
    return jax.shard_map(
        local,
        mesh=mesh,
        in_specs=(
            P(("dp", "seq"), None),
            P(("dp", "seq"), None),
            P(("dp", "seq"), None),
            P(("dp", "seq"), None),
            P(("dp", "seq"), None),
        ),
        out_specs=(P(("dp", "seq"), None), P(("dp", "seq"), None), P()),
        check_vma=False,
    )
```

profile of v0, /device:TPU:32, one launch (start us, length us, event | category | flops | bytes accessed | tf_op | source)
XLA Modules:
  0.0 553.2 jit_solution(16752581416438880143)
XLA Ops:
  7.2 2.4 reshape.64
  14.5 9.0 %while.11 = (s32[]{:T(128)}, bf16[4,4,128,240]{2,3,1,0:T(8,128)(2,1)}, bf16[4,4,128,240]{2,3,1,0:T(8,128)(2,1)S(1)}, bf16[4,4,128,80]{2,3,1,0:T(8,128)(2,1)S(1)}, s32[128]{0:T(128)S(1)}, /*index=5*/s32[]{:T(128)}) while((s32[]{:T(128)}, bf16[4,4,128,240]{2,3,1,0:T(8,128)(2,1)}, bf16[4,4,128,240]{2,3,1,0:T(8,128)(2,1)S(1)}, ...), condition=%wide.region_16.17_spmd.clone, body=%wide.region_12.16_spmd.clone.sunk | while | flops 64781952 | bytes 3454037 | solution.py:149
  28.9 64.4 %all-gather.9.cloned.1.call-done = bf16[1024,16,80]{2,1,0:T(8,128)(2,1)} async-done(((bf16[64,16,80]{2,1,0:T(8,128)(2,1)}), bf16[1024,16,80]{2,1,0:T(8,128)(2,1)}) %all-gather.9.cloned.1.call-update) | async-done | bytes 2621456 | tf_op jit(solution)/shard_map/all_gather | solution.py:105
  93.3 5.2 fusion.165
  99.8 71.4 %all-gather.11.cloned.1.call-done = bf16[1024,16,80]{2,1,0:T(8,128)(2,1)} async-done(((bf16[64,16,80]{2,1,0:T(8,128)(2,1)}), bf16[1024,16,80]{2,1,0:T(8,128)(2,1)}) %all-gather.11.cloned.1.call-update) | async-done | bytes 2621456 | tf_op jit(solution)/shard_map/all_gather | solution.py:106
  171.3 5.6 %fusion.166 = (bf16[1024,4,80]{2,1,0:T(4,128)(2,1)}, bf16[1024,4,80]{2,1,0:T(4,128)(2,1)}, bf16[1024,4,80]{2,1,0:T(4,128)(2,1)}, bf16[1024,4,80]{2,1,0:T(4,128)(2,1)}) fusion(bf16[1024,16,80]{2,1,0:T(8,128)(2,1)} %all-gather.11.cloned.1.call-done), kind=kLoop, calls=%fused_computation.180 | loop fusion | bytes 5242880 | tf_op jit(solution)/shard_map/slice | solution.py:116
  178.4 2.3 copy.156
  188.5 85.1 %all-gather.7.cloned.1.call-done = bf16[1024,16,160]{2,1,0:T(8,128)(2,1)} async-done(((bf16[64,16,160]{2,1,0:T(8,128)(2,1)}), bf16[1024,16,160]{2,1,0:T(8,128)(2,1)}) %all-gather.7.cloned.1.call-update) | async-done | bytes 5242896 | tf_op jit(solution)/shard_map/all_gather | solution.py:60
  273.6 13.2 %fusion.164 = (bf16[1024,4,80]{2,1,0:T(4,128)(2,1)}, bf16[1024,4,80]{2,1,0:T(4,128)(2,1)}, bf16[1024,4,80]{2,1,0:T(4,128)(2,1)}, bf16[1024,4,80]{2,1,0:T(4,128)(...) fusion(bf16[1024,16,160]{2,1,0:T(8,128)(2,1)} %all-gather.7.clo, ...), kind=kLoop, calls=%fused_computation.178 | loop fusion | bytes 10485760 | tf_op jit(solution)/shard_map/slice | solution.py:72
  286.8 2.3 copy.140
  291.4 2.3 copy.138
  301.6 2.3 copy.142
  304.0 2.5 fusion.91
  306.5 2.8 fusion.95
  309.3 2.3 copy.148
  311.7 2.3 copy.144
  314.0 2.3 copy.146
  324.1 2.3 copy.150
  326.5 2.5 fusion.93
  329.0 2.8 fusion.97
  336.2 104.7 %psum.7 = f32[1280]{0:T(1024)} all-reduce(f32[1280]{0:T(1024)S(1)} %add.12), channel_id=1, replica_groups=mesh['dp'=32,'seq'=16] {'dp','seq'}, use_global_device_ids=true, to_apply=%region_19.20 | all-reduce | flops 1280 | bytes 10240 | tf_op jit(solution)/shard_map/psum | solution.py:155
  440.9 28.0 %all-gather.2 = f32[16,64,16]{1,2,0:T(8,128)S(1)} all-gather(f32[1,64,16]{1,2,0:T(8,128)S(1)} %maximum_bitcast_fusion.3), channel_id=1, replica_groups=mesh['dp'=32,'seq'=16] {'seq'}, dimensions={0}, use_global_device_ids=true | all-gather | bytes 69632 | tf_op jit(solution)/shard_map/all_gather | solution.py:103
  469.7 28.8 %all-gather.1 = f32[16,64,16]{1,2,0:T(8,128)S(1)} all-gather(f32[1,64,16]{1,2,0:T(8,128)} %maximum_bitcast_fusion.2), channel_id=1, replica_groups=mesh['dp'=32,'seq'=16] {'seq'}, dimensions={0}, use_global_device_ids=true | all-gather | bytes 69632 | tf_op jit(solution)/shard_map/all_gather | solution.py:102
  499.2 27.6 %all-gather = f32[16,64,16]{1,2,0:T(8,128)S(1)} all-gather(f32[1,64,16]{1,2,0:T(8,128)} %maximum_bitcast_fusion.1), channel_id=1, replica_groups=mesh['dp'=32,'seq'=16] {'seq'}, dimensions={0}, use_global_device_ids=true | all-gather | bytes 69632 | tf_op jit(solution)/shard_map/all_gather | solution.py:101
  (185 shorter events, 72.8 us)
Async XLA Ops:
  7.2 6.5 %copy-start.8 = (bf16[128,3840]{1,0:T(8,128)(2,1)S(1)}, bf16[128,3840]{1,0:T(8,128)(2,1)}, u32[]{:S(2)}) copy-start(bf16[128,3840]{1,0:T(8,128)(2,1)} %param.9) | copy-start | bytes 2949124
  7.2 7.1 %copy-start.11 = (bf16[128,1280]{1,0:T(8,128)(2,1)S(1)}, bf16[128,1280]{1,0:T(8,128)(2,1)}, u32[]{:S(2)}) copy-start(bf16[128,1280]{1,0:T(8,128)(2,1)} %param.10) | copy-start | bytes 983044
  7.2 7.3 %copy-start.29 = (s32[1,128]{1,0:T(1,128)S(1)}, s32[1,128]{1,0:T(1,128)}, u32[]{:S(2)}) copy-start(s32[1,128]{1,0:T(1,128)} %param.11) | copy-start | bytes 1540
  7.2 86.1 %all-gather.9.cloned.1.call-start = ((), (), s32[]{:S(2)}) async-start(), calls=%async_computation.1 | async-start | bytes 4456448 | tf_op jit(solution)/shard_map/all_gather | solution.py:105
  10.4 160.9 %all-gather.11.cloned.1.call-start = ((), (), s32[]{:S(2)}) async-start(), calls=%async_computation.2 | async-start | bytes 4456448 | tf_op jit(solution)/shard_map/all_gather | solution.py:106
  12.5 261.1 %all-gather.7.cloned.1.call-start = ((), (), s32[]{:S(2)}) async-start(), calls=%async_computation | async-start | bytes 8912896 | tf_op jit(solution)/shard_map/all_gather | solution.py:60
  14.5 12.4 %copy-start.7 = (bf16[64,16,80]{2,1,0:T(8,128)(2,1)S(1)}, bf16[64,16,80]{2,1,0:T(8,128)(2,1)}, u32[]{:S(2)}) copy-start(bf16[64,16,80]{2,1,0:T(8,128)(2,1)} %reshape.65) | copy-start | bytes 491524
  293.8 4.5 copy-start.9
  293.8 4.5 copy-start.28
  295.3 4.1 copy-start.3
  295.3 11.1 %copy-start.30 = (f32[4,64]{1,0:T(4,128)}, f32[4,64]{1,0:T(4,128)S(1)}, u32[]{:S(2)}) copy-start(f32[4,64]{1,0:T(4,128)S(1)} %get-tuple-element.113) | copy-start | bytes 3076
  297.2 4.4 copy-start.31
  301.6 33.6 %copy-start.17 = (bf16[64,4,80]{2,0,1:T(8,128)(2,1)}, bf16[64,4,80]{2,0,1:T(8,128)(2,1)S(1)}, u32[]{:S(2)}) copy-start(bf16[64,4,80]{2,0,1:T(8,128)(2,1)S(1)} %fusion.94) | copy-start | bytes 122884
  301.6 4.8 copy-start.39
  316.3 4.5 copy-start.10
  316.3 4.5 copy-start.26
  317.8 4.1 copy-start.2
  317.8 11.2 %copy-start.32 = (f32[4,64]{1,0:T(4,128)}, f32[4,64]{1,0:T(4,128)S(1)}, u32[]{:S(2)}) copy-start(f32[4,64]{1,0:T(4,128)S(1)} %get-tuple-element.109) | copy-start | bytes 3076
  319.7 4.4 copy-start.33
  324.1 11.1 %copy-start.21 = (bf16[64,4,80]{2,0,1:T(8,128)(2,1)}, bf16[64,4,80]{2,0,1:T(8,128)(2,1)S(1)}, u32[]{:S(2)}) copy-start(bf16[64,4,80]{2,0,1:T(8,128)(2,1)S(1)} %fusion.96) | copy-start | bytes 122884
  324.1 4.9 copy-start.41
  326.5 8.7 %copy-start.19 = (bf16[64,4,80]{2,0,1:T(8,128)(2,1)S(1)}, bf16[64,4,80]{2,0,1:T(8,128)(2,1)}, u32[]{:S(2)}) copy-start(bf16[64,4,80]{2,0,1:T(8,128)(2,1)} %fusion.95) | copy-start | bytes 122884
  527.6 5.3 copy-start.36
  527.6 5.3 copy-start.37
  (21 other events, 46.0 us)
Sparse Core Ops, SparseCore 0:
  10.5 82.7 all-gather.8
  96.0 75.2 all-gather.10
  173.4 100.2 all-gather.6
where the time goes:
time: 554 us; the launch traced here: 553 us
  waiting for transfers between devices  221 us (40%)
  blocking collectives  189 us (34%)
  local copies, waits for them, and re-layouts  73.2 us (13%)
  matrix products  44.1 us (8%)
  between operations  14.4 us (3%)
  other arithmetic  11.1 us (2%)
    psum x1, blocking collectives, local(): bias_grad = lax.psum(local_sum, ('dp', 'seq'))  105 us
    all_gather x1, waiting for transfers between devices, local(): whole = lax.all_gather(packed[..., HEAD:], 'seq', axis=0, tiled=True)  85.1 us
    all_gather x1, waiting for transfers between devices, local(): grad_piece = lax.all_gather(grads, 'seq', axis=0, tiled=True)  71.4 us
    all_gather x1, waiting for transfers between devices, local(): query_piece = lax.all_gather(query_own, 'seq', axis=0, tiled=True)  64.4 us
    unnamed x106, local copies, waits for them, and re-layouts  37.1 us
    all_gather x1, blocking collectives, local(): lax.all_gather(jnp.concatenate(totals, axis=0), 'seq', axis=1, tiled=True)  28.8 us
    all_gather x1, blocking collectives, local(): lax.all_gather(jnp.concatenate(deltas, axis=0), 'seq', axis=1, tiled=True)  28 us
    all_gather x1, blocking collectives, local(): lax.all_gather(jnp.concatenate(tops, axis=0), 'seq', axis=1, tiled=True)  27.6 us
  transfers between devices with their start and end apart: 3, of which 3 were waited for; matrix products, arithmetic and copies ran while one was open for 8% of the time, Pallas kernels for 0%

commit v1 on v0

v1 whole, which is shorter than its diff:
```python
import functools

import jax
import jax.numpy as jnp
from jax import lax
from jax.experimental import pallas as pl
from jax.experimental.pallas import tpu as pltpu
from jax.sharding import PartitionSpec as P

HEAD = 80
HEADS = 16
SCALE = HEAD ** (-0.5)
LANES = 128
IN_ROWS = 2 * HEAD
OUT_ROWS = 3 * HEAD // 2
SUM_ROWS = 8
BLOCK = 256
F32 = jnp.float32
BF16 = jnp.bfloat16


def dot(left, right, left_dim, right_dim):
    return lax.dot_general(
        left, right, (((left_dim,), (right_dim,)), ((), ())), preferred_element_type=F32
    )


def params(mebibytes):
    return pltpu.CompilerParams(vmem_limit_bytes=mebibytes * 1024 * 1024)


def vmem(count):
    return [pl.BlockSpec(memory_space=pltpu.VMEM)] * count


def pack_kernel(qkv_ref, grad_ref, out_ref):
    qkv = qkv_ref[...].T
    grad = grad_ref[...].T
    for head in range(HEADS):
        first = 3 * HEAD * head
        left = qkv[first : first + 2 * HEAD]
        right = jnp.concatenate(
            [qkv[first + 2 * HEAD : first + 3 * HEAD], grad[HEAD * head : HEAD * (head + 1)]], axis=0
        )
        out_ref[head] = jnp.concatenate([left, right], axis=1)


def slopes_of(scores, upstream):
    exponent = jnp.exp(scores - jnp.max(scores, axis=0, keepdims=True))
    probs = exponent * (1.0 / jnp.sum(exponent, axis=0, keepdims=True))
    delta = jnp.sum(probs * upstream, axis=0, keepdims=True)
    return probs.astype(BF16), (probs * (upstream - delta)).astype(BF16)


def small_kernel(qkv_ref, grad_ref, ids_ref, out_ref, sum_ref, qkv_t, grad_t, out_t):
    qkv_t[...] = qkv_ref[...].T
    grad_t[...] = grad_ref[...].T
    rows = qkv_ref.shape[0]
    ids = jnp.broadcast_to(ids_ref[...].astype(F32), (rows, rows))
    allowed = ids == ids.T
    ones = jnp.ones((8, rows), BF16)
    sum_ref[...] = jnp.zeros_like(sum_ref)
    for head in range(HEADS):
        first = 3 * HEAD * head
        query = qkv_t[first : first + HEAD]
        key = qkv_t[first + HEAD : first + 2 * HEAD]
        value = qkv_t[first + 2 * HEAD : first + 3 * HEAD]
        grad = grad_t[HEAD * head : HEAD * (head + 1)]
        scores = jnp.where(allowed, dot(key, query, 0, 0) * SCALE, -1e30)
        weights, slopes = slopes_of(scores, dot(value, grad, 0, 0))
        query_grad = (dot(key, slopes, 1, 0) * SCALE).astype(BF16)
        out_t[first : first + HEAD] = query_grad
        out_t[first + HEAD : first + 2 * HEAD] = (dot(query, slopes, 1, 1) * SCALE).astype(BF16)
        out_t[first + 2 * HEAD : first + 3 * HEAD] = dot(grad, weights, 1, 1).astype(BF16)
        sum_ref[head : head + 1, :HEAD] = dot(ones, query_grad, 1, 1)[:1]
    out_ref[...] = out_t[...].T


def thirds(row):
    high = row.astype(BF16)
    rest = row - high.astype(F32)
    middle = rest.astype(BF16)
    low = (rest - middle.astype(F32)).astype(BF16)
    return [high.astype(F32), middle.astype(F32), low.astype(F32)]


def big_kernel(in_ref, sums_ref, out_ref, feat, key_sum, value_sum, query_t):
    pairs = in_ref.shape[0] // 2
    half = LANES // 2
    for pair in range(pairs):
        one, two = in_ref[2 * pair], in_ref[2 * pair + 1]
        columns = slice(LANES * pair, LANES * (pair + 1))
        feat[:IN_ROWS, columns] = jnp.concatenate([one[:, :half], two[:, :half]], axis=1)
        feat[IN_ROWS:, columns] = jnp.concatenate([one[:, half:], two[:, half:]], axis=1)
    key = feat[HEAD : 2 * HEAD]
    key_rows = key.T
    value_rows = feat[2 * HEAD : 3 * HEAD].T
    length = key.shape[1]
    for start in range(0, length, BLOCK):
        columns = slice(start, start + BLOCK)
        query = feat[:HEAD, columns]
        grad = feat[3 * HEAD :, columns]
        scores = dot(key_rows, query, 1, 0) * SCALE
        weights, slopes = slopes_of(scores, dot(value_rows, grad, 1, 0))
        query_t[:, columns] = (dot(key, slopes, 1, 0) * SCALE).astype(BF16)
        key_part = dot(slopes, query.T, 1, 0)
        value_part = dot(weights, grad.T, 1, 0)
        if start == 0:
            key_sum[...] = key_part
            value_sum[...] = value_part
        else:
            key_sum[...] += key_part
            value_sum[...] += value_part
    query_grad = query_t[...]
    big_row = dot(jnp.ones((8, length), BF16), query_grad, 1, 1)[:1]
    big_row = jnp.concatenate([big_row, jnp.zeros((1, LANES - HEAD), F32)], axis=1)
    extra = jnp.concatenate(
        thirds(big_row) + thirds(sums_ref[...]) + [jnp.zeros((2, LANES), F32)], axis=0
    )
    whole = jnp.concatenate(
        [query_grad.astype(F32), (key_sum[...] * SCALE).T, value_sum[...].T], axis=0
    )
    for pair in range(pairs):
        block = whole[:, LANES * pair : LANES * (pair + 1)]
        upper, lower = block[:OUT_ROWS], block[OUT_ROWS:]
        one = jnp.concatenate([upper[:, :half], lower[:, :half]], axis=1)
        two = jnp.concatenate([upper[:, half:], lower[:, half:]], axis=1)
        out_ref[2 * pair] = jnp.concatenate([one, extra], axis=0).astype(BF16)
        out_ref[2 * pair + 1] = jnp.concatenate([two, extra], axis=0).astype(BF16)


def unpack_kernel(in_ref, out_ref):
    half = LANES // 2
    parts = []
    for head in range(HEADS):
        block = in_ref[head].astype(F32)[:OUT_ROWS]
        parts.append(jnp.concatenate([block[:, :half], block[:, half:]], axis=0).astype(BF16))
    out_ref[...] = jnp.concatenate(parts, axis=0).T


def call(kernel, shapes, count, scratch=(), mebibytes=32, flops=0, name=None):
    outs = vmem(len(shapes))
    return pl.pallas_call(
        kernel,
        out_shape=shapes if len(shapes) > 1 else shapes[0],
        in_specs=vmem(count),
        out_specs=outs if len(shapes) > 1 else outs[0],
        scratch_shapes=scratch,
        compiler_params=params(mebibytes),
        cost_estimate=pl.CostEstimate(flops=flops, bytes_accessed=2**20, transcendentals=0),
        name=name,
    )


def local(big_qkv, big_grad, small_qkv, small_grad, small_ids):
    rows = big_qkv.shape[0]
    small_rows = small_qkv.shape[0]
    images = lax.axis_size("dp")
    parts = lax.axis_size("seq")
    length = rows * parts
    width = 3 * HEAD * HEADS
    image = lax.axis_index("dp")

    sent = call(
        pack_kernel, [jax.ShapeDtypeStruct((HEADS, IN_ROWS, LANES), BF16)], 2, name="pack"
    )(big_qkv, big_grad)
    got = lax.all_to_all(sent, "seq", 0, 0, tiled=True)

    small_out, small_sum = call(
        small_kernel,
        [
            jax.ShapeDtypeStruct((small_rows, width), BF16),
            jax.ShapeDtypeStruct((HEADS, LANES), F32),
        ],
        3,
        [
            pltpu.VMEM((width, small_rows), BF16),
            pltpu.VMEM((HEAD * HEADS, small_rows), BF16),
            pltpu.VMEM((width, small_rows), BF16),
        ],
        flops=10**10,
        name="small",
    )(small_qkv, small_grad, small_ids)
    share = HEADS * LANES // images
    of_all = jnp.sum(lax.all_gather(small_sum, "dp", axis=0), axis=0).reshape(images, share)
    mine = lax.dynamic_index_in_dim(of_all, image, 0, keepdims=True)
    mine = jnp.concatenate([mine, jnp.zeros((1, LANES - share), F32)], axis=1)

    back = call(
        big_kernel,
        [jax.ShapeDtypeStruct((parts, OUT_ROWS + SUM_ROWS, LANES), BF16)],
        2,
        [
            pltpu.VMEM((4 * HEAD, length), BF16),
            pltpu.VMEM((length, HEAD), F32),
            pltpu.VMEM((length, HEAD), F32),
            pltpu.VMEM((HEAD, length), BF16),
        ],
        mebibytes=48,
        flops=10**10,
        name="big",
    )(got, mine)
    home = lax.all_to_all(back, "seq", 0, 0, tiled=True)

    extra = home[:, OUT_ROWS : OUT_ROWS + 6].astype(F32)
    big_sum = extra[:, 0] + extra[:, 1] + extra[:, 2]
    share_sum = jnp.sum(extra[:, 3] + extra[:, 4] + extra[:, 5], axis=0)[:share]
    total = big_sum.reshape(images, share) + jnp.where(
        jnp.arange(images)[:, None] == image, share_sum[None], 0.0
    )
    total = total.reshape(1, 1, HEADS * LANES)
    everyone = lax.all_to_all(
        jnp.broadcast_to(total, (images, 1, HEADS * LANES)), "dp", 0, 0, tiled=True
    )
    bias_grad = jnp.sum(everyone, axis=0).reshape(HEADS, LANES)[:, :HEAD].reshape(HEADS * HEAD)

    big_out = call(
        unpack_kernel, [jax.ShapeDtypeStruct((rows, width), BF16)], 1, flops=10**9, name="unpack"
    )(home)
    return big_out, small_out, bias_grad


def solution(mesh):
    spec = P(("dp", "seq"), None)
    return jax.shard_map(
        local,
        mesh=mesh,
        in_specs=(spec,) * 5,
        out_specs=(spec, spec, P()),
        check_vma=False,
    )
```

time: 554 us -> 118 us (0.21)
  the two profiles are of different devices: /device:TPU:32 before, /device:TPU:1 now
where the time goes in v1:
time: 118 us
  starting transfers between devices  39.3 us (33%)
  waiting for transfers between devices  30.7 us (26%)
  blocking collectives  25.8 us (22%)
  Pallas kernels  16.6 us (14%)
  local copies, waits for them, and re-layouts  4.24 us (4%)
    all_gather x1, blocking collectives, local(): lax.all_gather(small_sum, 'dp', axis=0)  25.8 us
    all_to_all x1, waiting for transfers between devices, local(): home = lax.all_to_all(back, 'seq', 0, 0, tiled=True)  23 us
    all_to_all x1, starting transfers between devices, local(): got = lax.all_to_all(sent, 'seq', 0, 0, tiled=True)  15.9 us
    all_to_all x1, starting transfers between devices, local(): home = lax.all_to_all(back, 'seq', 0, 0, tiled=True)  11.7 us
    all_to_all x1, starting transfers between devices, local(): lax.all_to_all(jnp.broadcast_to(total, (images, 1, HEADS * LANES)), 'dp',...  11.7 us
    all_to_all x1, waiting for transfers between devices, local(): lax.all_to_all(jnp.broadcast_to(total, (images, 1, HEADS * LANES)), 'dp',...  7.68 us
    pallas_call x1, Pallas kernels, local(): call(small_kernel, [jax.ShapeDtypeStruct((small_rows, width), BF16), jax....  7.35 us
    pallas_call x1, Pallas kernels, local(): call(big_kernel, [jax.ShapeDtypeStruct((parts, OUT_ROWS + SUM_ROWS, LANES...  6.56 us
  transfers between devices with their start and end apart: 3, of which 2 were waited for; matrix products, arithmetic and copies ran while one was open for 0% of the time, Pallas kernels for 7%

profile of v1, /device:TPU:1, one launch (start us, length us, event | category | flops | bytes accessed | tf_op | source)
XLA Modules:
  0.0 117.7 jit_solution(7920890439433045796)
XLA Ops:
  0.6 0.0 copy-start
  0.6 1.0 copy-done
  1.7 0.9 copy-done.1
  2.6 1.4 %pack.1 = bf16[16,160,128]{2,1,0:T(8,128)(2,1)} custom-call(bf16[64,3840]{1,0:T(8,128)(2,1)S(1)} %copy-done, bf16[64,1280]{1,0:T(8,128)(2,1)S(1)} %copy-done.1), custom_call_target="tpu_custom_call" | custom-call | bytes 1048576 | tf_op jit(solution)/shard_map/pack/pallas_call | solution.py:164
  4.0 15.9 %all-to-all-start = ((bf16[16,160,128]{2,1,0:T(8,128)(2,1)}), bf16[16,160,128]{2,1,0:T(8,128)(2,1)S(1)}, u32[]{:S(2)}, u32[]{:S(2)}) async-start(bf16[16,160,128]{2,1,0:T(8,128)(2,1)} %pack.1), calls=%async_computation | async-start | bytes 1310720 | tf_op jit(solution)/shard_map/all_to_all | solution.py:167
  19.9 0.0 copy-start.4
  19.9 0.0 copy-done.2
  19.9 0.6 copy-done.4
  20.6 7.4 %small.1 = (bf16[128,3840]{1,0:T(8,128)(2,1)}, f32[16,128]{1,0:T(8,128)S(1)}) custom-call(bf16[128,3840]{1,0:T(8,128)(2,1)S(1)} %copy-done.2, bf16[128,1280]{1,0:T(8,128)(2,1)S(1)} %copy-done.3, s32[1,128]{1,0:T(1,128)S(1)} %copy-done.4), custom_call_target="tpu_custom_call" | custom-call | flops 10000000000 | bytes 1048576 | tf_op jit(solution)/shard_map/small/pallas_call | solution.py:169
  27.9 25.8 %all-gather = f32[512,128]{1,0:T(8,128)S(1)} all-gather(f32[16,128]{1,0:T(8,128)S(1)} %get-tuple-element.5), channel_id=2, replica_groups=mesh['dp'=32,'seq'=16] {'dp'}, dimensions={0}, use_global_device_ids=true | all-gather | bytes 270336 | tf_op jit(solution)/shard_map/all_gather | solution.py:185
  53.8 0.1 reshape.64
  53.9 0.0 all-to-all-done.in_ref
  53.9 6.6 %big.1 = bf16[16,128,128]{2,1,0:T(8,128)(2,1)} custom-call(bf16[16,160,128]{2,1,0:T(8,128)(2,1)S(1)} %all-to-all-done.in_ref, f32[1,128]{1,0:T(1,128)S(1)} %concatenate.3.sums_ref), custom_call_target="tpu_custom_call" | custom-call | flops 10000000000 | bytes 1048576 | tf_op jit(solution)/shard_map/big/pallas_call | solution.py:189
  60.5 11.7 %all-to-all-start.1 = ((bf16[16,128,128]{2,1,0:T(8,128)(2,1)}), bf16[16,128,128]{2,1,0:T(8,128)(2,1)S(1)}, u32[]{:S(2)}, u32[]{:S(2)}) async-start(bf16[16,128,128]{2,1,0:T(8,128)(2,1)} %big.1), calls=%async_computation.1 | async-start | bytes 1048576 | tf_op jit(solution)/shard_map/all_to_all | solution.py:203
  72.2 23.0 %all-to-all-done.1.in_ref = bf16[16,128,128]{2,1,0:T(8,128)(2,1)S(1)} async-done(((bf16[16,128,128]{2,1,0:T(8,128)(2,1)}), bf16[16,128,128]{2,1,0:T(8,128)(2,1)S(1)}, u32[]{:S(2)}, u32[]{:S(2)}) %all-to-all-start.1) | async-done | bytes 524320 | tf_op jit(solution)/shard_map/all_to_all | solution.py:203
  95.2 0.1 fusion
  95.3 0.1 broadcast_select_fusion
  95.4 0.1 select_n.17
  95.5 0.8 broadcast_in_dim.31
  96.3 11.7 %all-to-all-start.2 = ((f32[32,1,2048]{2,1,0:T(1,128)}), f32[32,1,2048]{2,1,0:T(1,128)S(1)}, u32[]{:S(2)}, u32[]{:S(2)}) async-start(f32[32,1,2048]{2,1,0:T(1,128)} %broadcast_in_dim.31), calls=%async_computation.2 | async-start | bytes 524288 | tf_op jit(solution)/shard_map/all_to_all | solution.py:212
  108.0 1.2 %unpack.1 = bf16[64,3840]{1,0:T(8,128)(2,1)} custom-call(bf16[16,128,128]{2,1,0:T(8,128)(2,1)S(1)} %all-to-all-done.1.in_ref), custom_call_target="tpu_custom_call" | custom-call | flops 1000000000 | bytes 1048576 | tf_op jit(solution)/shard_map/unpack/pallas_call | solution.py:217
  109.2 7.7 %all-to-all-done.2 = f32[32,1,2048]{2,1,0:T(1,128)S(1)} async-done(((f32[32,1,2048]{2,1,0:T(1,128)}), f32[32,1,2048]{2,1,0:T(1,128)S(1)}, u32[]{:S(2)}, u32[]{:S(2)}) %all-to-all-start.2) | async-done | bytes 262176 | tf_op jit(solution)/shard_map/all_to_all | solution.py:212
  116.9 0.2 reduce_sum.29
  117.1 0.7 reshape.66
  (10 shorter events, 0.1 us)
Async XLA Ops:
  0.6 1.0 copy-start
  1.7 0.9 copy-start.1
  4.0 15.9 %copy-start.2 = (bf16[128,3840]{1,0:T(8,128)(2,1)S(1)}, bf16[128,3840]{1,0:T(8,128)(2,1)}, u32[]{:S(2)}) copy-start(bf16[128,3840]{1,0:T(8,128)(2,1)} %qkv_ref.3) | copy-start | bytes 2949124
  4.0 15.9 %copy-start.3 = (bf16[128,1280]{1,0:T(8,128)(2,1)S(1)}, bf16[128,1280]{1,0:T(8,128)(2,1)}, u32[]{:S(2)}) copy-start(bf16[128,1280]{1,0:T(8,128)(2,1)} %grad_ref.3) | copy-start | bytes 983044
  4.0 49.9 %all-to-all-start = ((bf16[16,160,128]{2,1,0:T(8,128)(2,1)}), bf16[16,160,128]{2,1,0:T(8,128)(2,1)S(1)}, u32[]{:S(2)}, u32[]{:S(2)}) async-start(bf16[16,160,128]{2,1,0:T(8,128)(2,1)} %pack.1), calls=%async_computation | async-start | bytes 1310720 | tf_op jit(solution)/shard_map/all_to_all | solution.py:167
  19.9 0.7 copy-start.4
  60.5 34.8 %all-to-all-start.1 = ((bf16[16,128,128]{2,1,0:T(8,128)(2,1)}), bf16[16,128,128]{2,1,0:T(8,128)(2,1)S(1)}, u32[]{:S(2)}, u32[]{:S(2)}) async-start(bf16[16,128,128]{2,1,0:T(8,128)(2,1)} %big.1), calls=%async_computation.1 | async-start | bytes 1048576 | tf_op jit(solution)/shard_map/all_to_all | solution.py:203
  96.3 20.6 %all-to-all-start.2 = ((f32[32,1,2048]{2,1,0:T(1,128)}), f32[32,1,2048]{2,1,0:T(1,128)S(1)}, u32[]{:S(2)}, u32[]{:S(2)}) async-start(f32[32,1,2048]{2,1,0:T(1,128)} %broadcast_in_dim.31), calls=%async_computation.2 | async-start | bytes 524288 | tf_op jit(solution)/shard_map/all_to_all | solution.py:212

commit v2 on v1

--- a/solution.py
+++ b/solution.py
@@ -1,5 +1,3 @@
-import functools
-
 import jax
 import jax.numpy as jnp
 from jax import lax
@@ -14,6 +12,8 @@
 IN_ROWS = 2 * HEAD
 OUT_ROWS = 3 * HEAD // 2
 SUM_ROWS = 8
+STEPS = 2
+SHARE = HEADS * HEAD // 2**STEPS
 BLOCK = 256
 F32 = jnp.float32
 BF16 = jnp.bfloat16
@@ -29,11 +29,7 @@
     return pltpu.CompilerParams(vmem_limit_bytes=mebibytes * 1024 * 1024)
 
 
-def vmem(count):
-    return [pl.BlockSpec(memory_space=pltpu.VMEM)] * count
-
-
-def pack_kernel(qkv_ref, grad_ref, out_ref):
+def pack(qkv_ref, grad_ref, out_ref):
     qkv = qkv_ref[...].T
     grad = grad_ref[...].T
     for head in range(HEADS):
@@ -52,14 +48,21 @@
     return probs.astype(BF16), (probs * (upstream - delta)).astype(BF16)
 
 
-def small_kernel(qkv_ref, grad_ref, ids_ref, out_ref, sum_ref, qkv_t, grad_t, out_t):
-    qkv_t[...] = qkv_ref[...].T
-    grad_t[...] = grad_ref[...].T
-    rows = qkv_ref.shape[0]
+def small_images(qkv_hbm, grad_hbm, ids_ref, out_hbm, sum_ref, scratch):
+    qkv, grads, qkv_t, grad_t, out_t, out, query_t, sems = scratch
+    loads = [
+        pltpu.make_async_copy(qkv_hbm, qkv, sems.at[0]),
+        pltpu.make_async_copy(grad_hbm, grads, sems.at[1]),
+    ]
+    for load in loads:
+        load.start()
+    rows = qkv.shape[0]
     ids = jnp.broadcast_to(ids_ref[...].astype(F32), (rows, rows))
     allowed = ids == ids.T
-    ones = jnp.ones((8, rows), BF16)
-    sum_ref[...] = jnp.zeros_like(sum_ref)
+    for load in loads:
+        load.wait()
+    qkv_t[...] = qkv[...].T
+    grad_t[...] = grads[...].T
     for head in range(HEADS):
         first = 3 * HEAD * head
         query = qkv_t[first : first + HEAD]
@@ -70,18 +73,46 @@
         weights, slopes = slopes_of(scores, dot(value, grad, 0, 0))
         query_grad = (dot(key, slopes, 1, 0) * SCALE).astype(BF16)
         out_t[first : first + HEAD] = query_grad
+        query_t[HEAD * head : HEAD * (head + 1)] = query_grad
         out_t[first + HEAD : first + 2 * HEAD] = (dot(query, slopes, 1, 1) * SCALE).astype(BF16)
         out_t[first + 2 * HEAD : first + 3 * HEAD] = dot(grad, weights, 1, 1).astype(BF16)
-        sum_ref[head : head + 1, :HEAD] = dot(ones, query_grad, 1, 1)[:1]
-    out_ref[...] = out_t[...].T
-
-
-def thirds(row):
-    high = row.astype(BF16)
-    rest = row - high.astype(F32)
-    middle = rest.astype(BF16)
-    low = (rest - middle.astype(F32)).astype(BF16)
-    return [high.astype(F32), middle.astype(F32), low.astype(F32)]
+    out[...] = out_t[...].T
+    store = pltpu.make_async_copy(out, out_hbm, sems.at[0])
+    store.start()
+    sum_ref[...] = dot(jnp.ones((8, rows), BF16), query_t[...], 1, 1)[:1]
+    store.wait()
+
+
+def first_kernel(
+    core_ref, qkv_hbm, grad_hbm, small_qkv, small_grad, ids_ref, out_ref, small_out, sum_ref, qkv, grad, sems, *scratch
+):
+    loads = [
+        pltpu.make_async_copy(qkv_hbm, qkv, sems.at[0]),
+        pltpu.make_async_copy(grad_hbm, grad, sems.at[1]),
+    ]
+    for load in loads:
+        load.start()
+    for load in loads:
+        load.wait()
+    pack(qkv, grad, out_ref)
+    sum_ref[...] = jnp.zeros_like(sum_ref)
+
+    @pl.when(core_ref[0] == 1)
+    def _():
+        small_images(small_qkv, small_grad, ids_ref, small_out, sum_ref, scratch)
+
+
+def second_kernel(core_ref, small_qkv, small_grad, ids_ref, before, small_out, sum_ref, *scratch):
+    sum_ref[...] = jnp.zeros_like(sum_ref)
+
+    @pl.when(core_ref[0] == 0)
+    def _():
+        small_images(small_qkv, small_grad, ids_ref, small_out, sum_ref, scratch)
+
+
+def pieces(row):
+    high = row.astype(BF16).astype(F32)
+    return jnp.concatenate([high, (row - high).astype(BF16).astype(F32)], axis=0)
 
 
 def big_kernel(in_ref, sums_ref, out_ref, feat, key_sum, value_sum, query_t):
@@ -114,9 +145,7 @@
     query_grad = query_t[...]
     big_row = dot(jnp.ones((8, length), BF16), query_grad, 1, 1)[:1]
     big_row = jnp.concatenate([big_row, jnp.zeros((1, LANES - HEAD), F32)], axis=1)
-    extra = jnp.concatenate(
-        thirds(big_row) + thirds(sums_ref[...]) + [jnp.zeros((2, LANES), F32)], axis=0
-    )
+    extra = pieces(jnp.concatenate([sums_ref[...], big_row], axis=0))
     whole = jnp.concatenate(
         [query_grad.astype(F32), (key_sum[...] * SCALE).T, value_sum[...].T], axis=0
     )
@@ -138,18 +167,35 @@
     out_ref[...] = jnp.concatenate(parts, axis=0).T
 
 
-def call(kernel, shapes, count, scratch=(), mebibytes=32, flops=0, name=None):
-    outs = vmem(len(shapes))
+def call(kernel, shapes, in_specs, out_specs, operands, scratch=(), mebibytes=60, flops=0, name=None, aliases=None):
     return pl.pallas_call(
         kernel,
-        out_shape=shapes if len(shapes) > 1 else shapes[0],
-        in_specs=vmem(count),
-        out_specs=outs if len(shapes) > 1 else outs[0],
+        out_shape=shapes,
+        in_specs=in_specs,
+        out_specs=out_specs,
         scratch_shapes=scratch,
         compiler_params=params(mebibytes),
         cost_estimate=pl.CostEstimate(flops=flops, bytes_accessed=2**20, transcendentals=0),
+        input_output_aliases=aliases or {},
         name=name,
-    )
+    )(*operands)
+
+
+VMEM = pl.BlockSpec(memory_space=pltpu.VMEM)
+SMEM = pl.BlockSpec(memory_space=pltpu.SMEM)
+ANY = pl.BlockSpec(memory_space=pl.ANY)
+
+
+def halved(sums, image, images, core):
+    for step in range(STEPS):
+        bit = 2 << step
+        half = sums.shape[0] // 2
+        upper = (image // bit) % 2
+        kept = lax.dynamic_slice(sums, (upper * half,), (half,))
+        given = lax.dynamic_slice(sums, ((1 - upper) * half,), (half,))
+        pairs = [(at, at ^ bit) for at in range(images) if at % 2 == core]
+        sums = kept + lax.ppermute(given, "dp", pairs)
+    return sums
 
 
 def local(big_qkv, big_grad, small_qkv, small_grad, small_ids):
@@ -160,63 +206,91 @@
     length = rows * parts
     width = 3 * HEAD * HEADS
     image = lax.axis_index("dp")
-
-    sent = call(
-        pack_kernel, [jax.ShapeDtypeStruct((HEADS, IN_ROWS, LANES), BF16)], 2, name="pack"
-    )(big_qkv, big_grad)
+    core = jnp.reshape(image % 2, (1,)).astype(jnp.int32)
+
+    small_scratch = [
+        pltpu.VMEM((small_rows, width), BF16),
+        pltpu.VMEM((small_rows, HEAD * HEADS), BF16),
+        pltpu.VMEM((width, small_rows), BF16),
+        pltpu.VMEM((HEAD * HEADS, small_rows), BF16),
+        pltpu.VMEM((width, small_rows), BF16),
+        pltpu.VMEM((small_rows, width), BF16),
+        pltpu.VMEM((HEAD * HEADS, small_rows), BF16),
+        pltpu.SemaphoreType.DMA((2,)),
+    ]
+    small_shape = jax.ShapeDtypeStruct((small_rows, width), BF16)
+    sum_shape = jax.ShapeDtypeStruct((1, HEADS * HEAD), F32)
+    sent, small_out, small_sum = call(
+        first_kernel,
+        [jax.ShapeDtypeStruct((HEADS, IN_ROWS, LANES), BF16), small_shape, sum_shape],
+        [SMEM, ANY, ANY, ANY, ANY, VMEM],
+        [VMEM, ANY, VMEM],
+        (core, big_qkv, big_grad, small_qkv, small_grad, small_ids),
+        [
+            pltpu.VMEM((rows, width), BF16),
+            pltpu.VMEM((rows, HEAD * HEADS), BF16),
+            pltpu.SemaphoreType.DMA((2,)),
+            *small_scratch,
+        ],
+        name="pack",
+    )
+    late_sums = halved(small_sum.reshape(HEADS * HEAD), image, images, 1)
+    sent, late_sums = lax.optimization_barrier((sent, late_sums))
     got = lax.all_to_all(sent, "seq", 0, 0, tiled=True)
 
     small_out, small_sum = call(
-        small_kernel,
-        [
-            jax.ShapeDtypeStruct((small_rows, width), BF16),
-            jax.ShapeDtypeStruct((HEADS, LANES), F32),
-        ],
-        3,
-        [
-            pltpu.VMEM((width, small_rows), BF16),
-            pltpu.VMEM((HEAD * HEADS, small_rows), BF16),
-            pltpu.VMEM((width, small_rows), BF16),
-        ],
+        second_kernel,
+        [small_shape, sum_shape],
+        [SMEM, ANY, ANY, VMEM, ANY],
+        [ANY, VMEM],
+        (core, small_qkv, small_grad, small_ids, small_out),
+        small_scratch,
         flops=10**10,
         name="small",
-    )(small_qkv, small_grad, small_ids)
-    share = HEADS * LANES // images
-    of_all = jnp.sum(lax.all_gather(small_sum, "dp", axis=0), axis=0).reshape(images, share)
-    mine = lax.dynamic_index_in_dim(of_all, image, 0, keepdims=True)
-    mine = jnp.concatenate([mine, jnp.zeros((1, LANES - share), F32)], axis=1)
+        aliases={4: 0},
+    )
+
+    sums = late_sums + halved(small_sum.reshape(HEADS * HEAD), image, images, 0)
+    sums = jnp.pad(sums, (0, 3 * LANES - SHARE)).reshape(3, LANES)
 
     back = call(
         big_kernel,
-        [jax.ShapeDtypeStruct((parts, OUT_ROWS + SUM_ROWS, LANES), BF16)],
-        2,
-        [
+        jax.ShapeDtypeStruct((parts, OUT_ROWS + SUM_ROWS, LANES), BF16),
+        [VMEM, VMEM],
+        VMEM,
+        (got, sums),
+        mebibytes=40,
+        scratch=[
             pltpu.VMEM((4 * HEAD, length), BF16),
             pltpu.VMEM((length, HEAD), F32),
             pltpu.VMEM((length, HEAD), F32),
             pltpu.VMEM((HEAD, length), BF16),
         ],
-        mebibytes=48,
         flops=10**10,
         name="big",
-    )(got, mine)
+    )
     home = lax.all_to_all(back, "seq", 0, 0, tiled=True)
 
-    extra = home[:, OUT_ROWS : OUT_ROWS + 6].astype(F32)
-    big_sum = extra[:, 0] + extra[:, 1] + extra[:, 2]
-    share_sum = jnp.sum(extra[:, 3] + extra[:, 4] + extra[:, 5], axis=0)[:share]
-    total = big_sum.reshape(images, share) + jnp.where(
-        jnp.arange(images)[:, None] == image, share_sum[None], 0.0
-    )
-    total = total.reshape(1, 1, HEADS * LANES)
+    extra = home[:, OUT_ROWS:].astype(F32)
+    extra = extra[:, :4] + extra[:, 4:]
+    share = jnp.sum(extra[:, :3], axis=0).reshape(3 * LANES)[:SHARE]
+    held = jnp.arange(2**STEPS) == (image // 2 % 2) * 2 + image // 4 % 2
+    total = extra[:, 3, :HEAD].reshape(HEADS * HEAD) + jnp.where(held[:, None], share, 0.0).reshape(HEADS * HEAD)
     everyone = lax.all_to_all(
-        jnp.broadcast_to(total, (images, 1, HEADS * LANES)), "dp", 0, 0, tiled=True
-    )
-    bias_grad = jnp.sum(everyone, axis=0).reshape(HEADS, LANES)[:, :HEAD].reshape(HEADS * HEAD)
+        jnp.broadcast_to(total, (images, 1, HEADS * HEAD)), "dp", 0, 0, tiled=True
+    )
+    bias_grad = jnp.sum(everyone, axis=(0, 1))
 
     big_out = call(
-        unpack_kernel, [jax.ShapeDtypeStruct((rows, width), BF16)], 1, flops=10**9, name="unpack"
-    )(home)
+        unpack_kernel,
+        jax.ShapeDtypeStruct((rows, width), BF16),
+        [VMEM],
+        VMEM,
+        (home,),
+        mebibytes=32,
+        flops=10**9,
+        name="unpack",
+    )
     return big_out, small_out, bias_grad
 
 

time: 118 us -> 110 us (0.932)
  blocking collectives: 25.8 us -> 0 us
  waiting for transfers between devices: 30.7 us -> 46.4 us
  Pallas kernels: 16.6 us -> 19.3 us
  local copies, waits for them, and re-layouts: 4.24 us -> 2.54 us
    all_gather x1 -> x0, blocking collectives: 25.8 us -> none  [local(): lax.all_gather(small_sum, 'dp', axis=0)]
    all_to_all x1, waiting for transfers between devices: 0.01 us -> 17.1 us  [local(): got = lax.all_to_all(sent, 'seq', 0, 0, tiled=True)]
    ppermute x0 -> x4, starting transfers between devices: none -> 10.3 us  [halved(): sums = kept + lax.ppermute(given, 'dp', pairs)]
    all_to_all x1, starting transfers between devices: 11.7 us -> 6.12 us  [local(): home = lax.all_to_all(back, 'seq', 0, 0, tiled=True)]
    all_to_all x1, starting transfers between devices: 11.7 us -> 7.21 us  [local(): lax.all_to_all(jnp.broadcast_to(total, (images, 1, HEADS * HEAD)), 'dp',...]
    pallas_call x4, Pallas kernels: 16.6 us -> 19.3 us  [call(): pl.pallas_call(kernel, out_shape=shapes, in_specs=in_specs, out_specs=out...]
    unnamed x10 -> x0, local copies, waits for them, and re-layouts: 2.58 us -> none
    all_to_all x1, waiting for transfers between devices: 23 us -> 20.6 us  [local(): home = lax.all_to_all(back, 'seq', 0, 0, tiled=True)]
  transfers between devices with their start and end apart: 3 -> 7, of which waited for: 2 -> 5; matrix products, arithmetic and copies ran while one was open for 0% -> 1% of each run, Pallas kernels for 7% -> 2%
where the time goes in v2:
time: 110 us; the launch traced here: 109 us
  waiting for transfers between devices  46.4 us (42%)
  starting transfers between devices  39.1 us (36%)
  Pallas kernels  19.3 us (18%)
  local copies, waits for them, and re-layouts  2.54 us (2%)
    all_to_all x1, waiting for transfers between devices, local(): home = lax.all_to_all(back, 'seq', 0, 0, tiled=True)  20.6 us
    pallas_call x4, Pallas kernels, call(): pl.pallas_call(kernel, out_shape=shapes, in_specs=in_specs, out_specs=out...  19.3 us
    all_to_all x1, waiting for transfers between devices, local(): got = lax.all_to_all(sent, 'seq', 0, 0, tiled=True)  17.1 us
    all_to_all x1, starting transfers between devices, local(): got = lax.all_to_all(sent, 'seq', 0, 0, tiled=True)  15.4 us
    ppermute x4, starting transfers between devices, halved(): sums = kept + lax.ppermute(given, 'dp', pairs)  10.3 us
    all_to_all x1, starting transfers between devices, local(): lax.all_to_all(jnp.broadcast_to(total, (images, 1, HEADS * HEAD)), 'dp',...  7.21 us
    all_to_all x1, waiting for transfers between devices, local(): lax.all_to_all(jnp.broadcast_to(total, (images, 1, HEADS * HEAD)), 'dp',...  6.72 us
    all_to_all x1, starting transfers between devices, local(): home = lax.all_to_all(back, 'seq', 0, 0, tiled=True)  6.12 us
  transfers between devices with their start and end apart: 7, of which 5 were waited for; matrix products, arithmetic and copies ran while one was open for 1% of the time, Pallas kernels for 2%

profile of v2, /device:TPU:1, one launch (start us, length us, event | category | flops | bytes accessed | tf_op | source)
XLA Modules:
  0.0 109.2 jit_solution(3954580173586857603)
XLA Ops:
  0.7 10.3 %pack.1 = (bf16[16,160,128]{2,1,0:T(8,128)(2,1)}, bf16[128,3840]{1,0:T(8,128)(2,1)}, f32[1,1280]{1,0:T(1,128)}) custom-call(s32[1]{0:T(128)} %bitcast.core_ref, bf16[64,3840]{1,0:T(8,128)(2,1)} %qkv_hbm.1, bf16[64,1280]{1,0:T(8,128)(2,1)} %grad_hbm.1, bf16[128,3840]{1,0:T(8,128)(2,1)} %small_qkv.3, bf16[128,1280]{1,0:T(8,128)(2,1)} %small_grad.3, ...), custom_call_target="tpu_custom_call" | custom-call | bytes 1048576 | tf_op jit(solution)/shard_map/pack/pallas_call | solution.py:171
  11.0 0.7 dynamic-slice_reduce_fusion.2
  11.7 3.9 %collective-permute-start = (f32[640]{0:T(1024)S(1)}, f32[640]{0:T(1024)S(1)}, u32[]{:S(2)}, u32[]{:S(2)}) collective-permute-start(f32[640]{0:T(1024)S(1)} %get-tuple-element.19), channel_id=1, source_target_pairs={{16,48},{48,16},{80,112},{112,80},{144,176},{176,144},{208,240},{2... | collective-permute-start | bytes 7688 | tf_op jit(solution)/shard_map/ppermute | solution.py:197
  15.7 0.9 collective-permute-done
  16.6 0.1 dynamic_slice.37
  16.7 4.9 %collective-permute-start.1 = (f32[320]{0:T(512)S(1)}, f32[320]{0:T(512)S(1)}, u32[]{:S(2)}, u32[]{:S(2)}) collective-permute-start(f32[320]{0:T(512)S(1)} %dynamic_slice.37), channel_id=1, source_target_pairs={{16,80},{48,112},{80,16},{112,48},{144,208},{176,240},{208,144},{2... | collective-permute-start | bytes 3848 | tf_op jit(solution)/shard_map/ppermute | solution.py:197
  21.6 1.0 collective-permute-done.1
  22.6 15.4 %all-to-all-start = ((bf16[16,160,128]{2,1,0:T(8,128)(2,1)}), bf16[16,160,128]{2,1,0:T(8,128)(2,1)S(1)}, u32[]{:S(2)}, u32[]{:S(2)}) async-start(bf16[16,160,128]{2,1,0:T(8,128)(2,1)} %get-tuple-element.12), calls=%async_computation | async-start | bytes 1310720 | tf_op jit(solution)/shard_map/all_to_all | solution.py:239
  38.1 1.3 %small.1 = (bf16[128,3840]{1,0:T(8,128)(2,1)}, f32[1,1280]{1,0:T(1,128)}) custom-call(s32[1]{0:T(128)} %bitcast.core_ref, bf16[128,3840]{1,0:T(8,128)(2,1)} %small_qkv.3, bf16[128,1280]{1,0:T(8,128)(2,1)} %small_grad.3, s32[1,128]{1,0:T(1,128)} %ids_ref.3, bf16[128,3840]{1,0:T(8,128)(2,1)} %get-tuple-element.14.before), custom_call_target="tpu_custom_call", output_to_operand_aliasing={{0}: (4, {})} | custom-call | flops 10000000000 | bytes 1048576 | tf_op jit(solution)/shard_map/small/pallas_call | solution.py:171
  39.3 0.7 dynamic-slice_reduce_fusion
  40.1 0.7 collective-permute-start.2
  40.8 0.1 dynamic_slice.43
  40.8 0.8 collective-permute-start.3
  41.7 0.1 add_add_fusion
  41.8 17.1 %all-to-all-done.in_ref = bf16[16,160,128]{2,1,0:T(8,128)(2,1)S(1)} async-done(((bf16[16,160,128]{2,1,0:T(8,128)(2,1)}), bf16[16,160,128]{2,1,0:T(8,128)(2,1)S(1)}, u32[]{:S(2)}, u32[]{:S(2)}) %all-to-all-start) | async-done | bytes 655392 | tf_op jit(solution)/shard_map/all_to_all | solution.py:239
  58.9 6.6 %big.1 = bf16[16,128,128]{2,1,0:T(8,128)(2,1)} custom-call(bf16[16,160,128]{2,1,0:T(8,128)(2,1)S(1)} %all-to-all-done.in_ref, f32[3,128]{1,0:T(4,128)S(1)} %pad_bitcast_fusion.sums_ref), custom_call_target="tpu_custom_call" | custom-call | flops 10000000000 | bytes 1048576 | tf_op jit(solution)/shard_map/big/pallas_call | solution.py:171
  65.4 6.1 %all-to-all-start.1 = ((bf16[16,128,128]{2,1,0:T(8,128)(2,1)}), bf16[16,128,128]{2,1,0:T(8,128)(2,1)S(1)}, u32[]{:S(2)}, u32[]{:S(2)}) async-start(bf16[16,128,128]{2,1,0:T(8,128)(2,1)} %big.1), calls=%async_computation.1 | async-start | bytes 1048576 | tf_op jit(solution)/shard_map/all_to_all | solution.py:272
  71.6 20.6 %all-to-all-done.1.in_ref = bf16[16,128,128]{2,1,0:T(8,128)(2,1)S(1)} async-done(((bf16[16,128,128]{2,1,0:T(8,128)(2,1)}), bf16[16,128,128]{2,1,0:T(8,128)(2,1)S(1)}, u32[]{:S(2)}, u32[]{:S(2)}) %all-to-all-start.1) | async-done | bytes 524320 | tf_op jit(solution)/shard_map/all_to_all | solution.py:272
  92.5 0.1 select_n.68
  92.6 0.7 broadcast_in_dim.23
  93.3 7.2 %all-to-all-start.2 = ((f32[32,1,1280]{2,1,0:T(1,128)}), f32[32,1,1280]{2,1,0:T(1,128)S(1)}, u32[]{:S(2)}, u32[]{:S(2)}) async-start(f32[32,1,1280]{2,1,0:T(1,128)} %broadcast_in_dim.23), calls=%async_computation.2 | async-start | bytes 327680 | tf_op jit(solution)/shard_map/all_to_all | solution.py:279
  100.5 1.2 %unpack.1 = bf16[64,3840]{1,0:T(8,128)(2,1)} custom-call(bf16[16,128,128]{2,1,0:T(8,128)(2,1)S(1)} %all-to-all-done.1.in_ref), custom_call_target="tpu_custom_call" | custom-call | flops 1000000000 | bytes 1048576 | tf_op jit(solution)/shard_map/unpack/pallas_call | solution.py:171
  101.8 6.7 %all-to-all-done.2 = f32[32,1,1280]{2,1,0:T(1,128)S(1)} async-done(((f32[32,1,1280]{2,1,0:T(1,128)}), f32[32,1,1280]{2,1,0:T(1,128)S(1)}, u32[]{:S(2)}, u32[]{:S(2)}) %all-to-all-start.2) | async-done | bytes 163872 | tf_op jit(solution)/shard_map/all_to_all | solution.py:279
  108.5 0.7 reduce_sum.19
  (14 shorter events, 0.3 us)
Async XLA Ops:
  11.7 4.9 %collective-permute-start = (f32[640]{0:T(1024)S(1)}, f32[640]{0:T(1024)S(1)}, u32[]{:S(2)}, u32[]{:S(2)}) collective-permute-start(f32[640]{0:T(1024)S(1)} %get-tuple-element.19), channel_id=1, source_target_pairs={{16,48},{48,16},{80,112},{112,80},{144,176},{176,144},{208,240},{2... | collective-permute-start | bytes 7688 | tf_op jit(solution)/shard_map/ppermute | solution.py:197
  16.7 5.9 %collective-permute-start.1 = (f32[320]{0:T(512)S(1)}, f32[320]{0:T(512)S(1)}, u32[]{:S(2)}, u32[]{:S(2)}) collective-permute-start(f32[320]{0:T(512)S(1)} %dynamic_slice.37), channel_id=1, source_target_pairs={{16,80},{48,112},{80,16},{112,48},{144,208},{176,240},{208,144},{2... | collective-permute-start | bytes 3848 | tf_op jit(solution)/shard_map/ppermute | solution.py:197
  22.6 36.3 %all-to-all-start = ((bf16[16,160,128]{2,1,0:T(8,128)(2,1)}), bf16[16,160,128]{2,1,0:T(8,128)(2,1)S(1)}, u32[]{:S(2)}, u32[]{:S(2)}) async-start(bf16[16,160,128]{2,1,0:T(8,128)(2,1)} %get-tuple-element.12), calls=%async_computation | async-start | bytes 1310720 | tf_op jit(solution)/shard_map/all_to_all | solution.py:239
  40.1 0.7 collective-permute-start.2
  40.8 0.8 collective-permute-start.3
  65.4 26.8 %all-to-all-start.1 = ((bf16[16,128,128]{2,1,0:T(8,128)(2,1)}), bf16[16,128,128]{2,1,0:T(8,128)(2,1)S(1)}, u32[]{:S(2)}, u32[]{:S(2)}) async-start(bf16[16,128,128]{2,1,0:T(8,128)(2,1)} %big.1), calls=%async_computation.1 | async-start | bytes 1048576 | tf_op jit(solution)/shard_map/all_to_all | solution.py:272
  93.3 15.2 %all-to-all-start.2 = ((f32[32,1,1280]{2,1,0:T(1,128)}), f32[32,1,1280]{2,1,0:T(1,128)S(1)}, u32[]{:S(2)}, u32[]{:S(2)}) async-start(f32[32,1,1280]{2,1,0:T(1,128)} %broadcast_in_dim.23), calls=%async_computation.2 | async-start | bytes 327680 | tf_op jit(solution)/shard_map/all_to_all | solution.py:279

commit v3 on v2

v3 whole, which is shorter than its diff:
```python
import math

import jax
import jax.numpy as jnp
from jax import lax
from jax.experimental import pallas as pl
from jax.experimental.pallas import tpu as pltpu
from jax.sharding import PartitionSpec as P

HEAD = 80
HEADS = 16
SCALE = HEAD ** (-0.5)
LANES = 128
IN_ROWS = 2 * HEAD
OUT_ROWS = 3 * HEAD // 2
SUM_ROWS = 8
STEPS = (((2, 2), (4, 4)), ((20, 4), (18, 2)))
SHARE = HEADS * HEAD // 4
EXPONENT = SCALE * math.log2(math.e)
F32 = jnp.float32
BF16 = jnp.bfloat16


def dot(left, right, left_dim, right_dim):
    return lax.dot_general(
        left, right, (((left_dim,), (right_dim,)), ((), ())), preferred_element_type=F32
    )


def params(mebibytes):
    return pltpu.CompilerParams(vmem_limit_bytes=mebibytes * 1024 * 1024)


def slopes_of(scores, upstream):
    exponent = jnp.exp2((scores - jnp.max(scores, axis=0, keepdims=True)) * EXPONENT)
    inverse = 1.0 / jnp.sum(exponent, axis=0, keepdims=True)
    delta = jnp.sum(exponent * upstream, axis=0, keepdims=True) * inverse
    probs = exponent * inverse
    return probs.astype(BF16), (probs * (upstream - delta)).astype(BF16)


def small_loads(qkv_hbm, grad_hbm, ids_hbm, scratch):
    sems = scratch[-1]
    sources = (qkv_hbm, grad_hbm, ids_hbm)
    return [pltpu.make_async_copy(sources[at], scratch[at], sems.at[at]) for at in range(3)]


def small_images(loads, out_hbm, kept_hbm, given_hbm, core, scratch):
    qkv, grads, ids_ref, qkv_t, grad_t, out_t, out, query_t, kept, given, sems = scratch
    rows = qkv.shape[0]
    for load in loads:
        load.wait()
    ids = jnp.broadcast_to(ids_ref[...].astype(F32), (rows, rows))
    allowed = ids == ids.T
    qkv_t[...] = qkv[...].T
    grad_t[...] = grads[...].T

    def part(head, which):
        first = 3 * HEAD * head + HEAD * which
        return qkv_t[first : first + HEAD]

    def grad(head):
        return grad_t[HEAD * head : HEAD * (head + 1)]

    heads = range(HEADS)
    scores = [jnp.where(allowed, dot(part(head, 1), part(head, 0), 0, 0), -1e30) for head in heads]
    upstream = [dot(part(head, 2), grad(head), 0, 0) for head in heads]
    both = [slopes_of(*pair) for pair in zip(scores, upstream)]
    query_grad = [(dot(part(head, 1), both[head][1], 1, 0) * SCALE).astype(BF16) for head in heads]
    key_grad = [(dot(part(head, 0), both[head][1], 1, 1) * SCALE).astype(BF16) for head in heads]
    value_grad = [dot(grad(head), both[head][0], 1, 1).astype(BF16) for head in heads]
    for head in heads:
        first = 3 * HEAD * head
        out_t[first : first + HEAD] = query_grad[head]
        query_t[HEAD * head : HEAD * (head + 1)] = query_grad[head]
        out_t[first + HEAD : first + 2 * HEAD] = key_grad[head]
        out_t[first + 2 * HEAD : first + 3 * HEAD] = value_grad[head]
    sums = dot(jnp.ones((8, rows), BF16), query_t[...], 1, 1)[:1]
    half = HEADS * HEAD // 2
    upper = lax.axis_index("dp") // STEPS[core][0][1] % 2
    kept[...] = jnp.where(upper == 1, sums[:, half:], sums[:, :half])
    given[...] = jnp.where(upper == 1, sums[:, :half], sums[:, half:])
    out[...] = out_t[...].T
    stores = [
        pltpu.make_async_copy(out, out_hbm, sems.at[0]),
        pltpu.make_async_copy(kept, kept_hbm, sems.at[1]),
        pltpu.make_async_copy(given, given_hbm, sems.at[2]),
    ]
    for store in stores:
        store.start()
    for store in stores:
        store.wait()


def first_kernel(
    qkv_hbm,
    grad_hbm,
    small_qkv,
    small_grad,
    ids_hbm,
    out_hbm,
    small_out,
    kept_hbm,
    given_hbm,
    qkv,
    grad,
    packed,
    in_sems,
    out_sems,
    *scratch,
):
    parts = in_sems.shape[1]
    heads = HEADS // parts
    wide, narrow = 3 * HEAD * heads, HEAD * heads
    loads = []
    for part in range(parts):
        columns = pl.ds(part * wide, wide)
        loads.append(
            pltpu.make_async_copy(qkv_hbm.at[:, columns], qkv.at[:, columns], in_sems.at[0, part])
        )
        columns = pl.ds(part * narrow, narrow)
        loads.append(
            pltpu.make_async_copy(grad_hbm.at[:, columns], grad.at[:, columns], in_sems.at[1, part])
        )
    for load in loads:
        load.start()
    late = lax.axis_index("dp") % 2 == 1
    after = small_loads(small_qkv, small_grad, ids_hbm, scratch)

    @pl.when(late)
    def _():
        for load in after:
            load.start()

    stores = []
    for part in range(parts):
        loads[2 * part].wait()
        loads[2 * part + 1].wait()
        turned = qkv[:, part * wide : (part + 1) * wide].T
        turned_grad = grad[:, part * narrow : (part + 1) * narrow].T
        for index in range(heads):
            first = 3 * HEAD * index
            left = turned[first : first + 2 * HEAD]
            right = jnp.concatenate(
                [
                    turned[first + 2 * HEAD : first + 3 * HEAD],
                    turned_grad[HEAD * index : HEAD * (index + 1)],
                ],
                axis=0,
            )
            packed[part * heads + index] = jnp.concatenate([left, right], axis=1)
        done = pl.ds(part * heads, heads)
        stores.append(pltpu.make_async_copy(packed.at[done], out_hbm.at[done], out_sems.at[part]))
        stores[-1].start()

    @pl.when(late)
    def _():
        small_images(after, small_out, kept_hbm, given_hbm, 1, scratch)

    for store in stores:
        store.wait()


def second_kernel(
    small_qkv, small_grad, ids_hbm, before, small_out, kept_hbm, given_hbm, *scratch
):
    @pl.when(lax.axis_index("dp") % 2 == 0)
    def _():
        loads = small_loads(small_qkv, small_grad, ids_hbm, scratch)
        for load in loads:
            load.start()
        small_images(loads, small_out, kept_hbm, given_hbm, 0, scratch)


def pieces(row):
    high = row.astype(BF16).astype(F32)
    return jnp.concatenate([high, (row - high).astype(BF16).astype(F32)], axis=0)


def big_kernel(in_ref, sums_ref, out_ref, feat):
    pairs = in_ref.shape[0] // 2
    half = LANES // 2
    for pair in range(pairs):
        one, two = in_ref[2 * pair], in_ref[2 * pair + 1]
        columns = slice(LANES * pair, LANES * (pair + 1))
        feat[:IN_ROWS, columns] = jnp.concatenate([one[:, :half], two[:, :half]], axis=1)
        feat[IN_ROWS:, columns] = jnp.concatenate([one[:, half:], two[:, half:]], axis=1)
    query, key, value, grad = (feat[HEAD * which : HEAD * (which + 1)] for which in range(4))
    length = key.shape[1]
    weights, slopes = slopes_of(dot(key.T, query, 1, 0), dot(value.T, grad, 1, 0))
    query_grad = (dot(key, slopes, 1, 0) * SCALE).astype(BF16)
    key_grad = dot(query, slopes, 1, 1) * SCALE
    value_grad = dot(grad, weights, 1, 1)
    big_row = dot(jnp.ones((8, length), BF16), query_grad, 1, 1)[:1]
    big_row = jnp.concatenate([big_row, jnp.zeros((1, LANES - HEAD), F32)], axis=1)
    extra = pieces(jnp.concatenate([sums_ref[...], big_row], axis=0))
    whole = jnp.concatenate([query_grad.astype(F32), key_grad, value_grad], axis=0)
    for pair in range(pairs):
        block = whole[:, LANES * pair : LANES * (pair + 1)]
        upper, lower = block[:OUT_ROWS], block[OUT_ROWS:]
        one = jnp.concatenate([upper[:, :half], lower[:, :half]], axis=1)
        two = jnp.concatenate([upper[:, half:], lower[:, half:]], axis=1)
        out_ref[2 * pair] = jnp.concatenate([one, extra], axis=0).astype(BF16)
        out_ref[2 * pair + 1] = jnp.concatenate([two, extra], axis=0).astype(BF16)


def unpack_kernel(in_ref, out_ref):
    half = LANES // 2
    parts = []
    for head in range(HEADS):
        block = in_ref[head].astype(F32)[:OUT_ROWS]
        parts.append(jnp.concatenate([block[:, :half], block[:, half:]], axis=0).astype(BF16))
    out_ref[...] = jnp.concatenate(parts, axis=0).T


def call(kernel, shapes, in_specs, out_specs, operands, scratch=(), mebibytes=60, flops=0, name=None, aliases=None):
    return pl.pallas_call(
        kernel,
        out_shape=shapes,
        in_specs=in_specs,
        out_specs=out_specs,
        scratch_shapes=scratch,
        compiler_params=params(mebibytes),
        cost_estimate=pl.CostEstimate(flops=flops, bytes_accessed=2**20, transcendentals=0),
        input_output_aliases=aliases or {},
        name=name,
    )(*operands)


VMEM = pl.BlockSpec(memory_space=pltpu.VMEM)
ANY = pl.BlockSpec(memory_space=pl.ANY)


def summed(kept, given, image, images, core):
    (first, _), (second, bit) = STEPS[core]
    pairs = [[(at, at ^ step) for at in range(images) if at % 2 == core] for step in (first, second)]
    sums = (kept + lax.ppermute(given, "dp", pairs[0])).reshape(2 * SHARE)
    upper = image // bit % 2
    kept = lax.dynamic_slice(sums, (upper * SHARE,), (SHARE,))
    given = lax.dynamic_slice(sums, ((1 - upper) * SHARE,), (SHARE,))
    sums = kept + lax.ppermute(given, "dp", pairs[1])
    return jnp.where(image % 2 == core, sums, 0.0)


def local(big_qkv, big_grad, small_qkv, small_grad, small_ids):
    rows = big_qkv.shape[0]
    small_rows = small_qkv.shape[0]
    images = lax.axis_size("dp")
    parts = lax.axis_size("seq")
    length = rows * parts
    width = 3 * HEAD * HEADS
    image = lax.axis_index("dp")

    small_scratch = [
        pltpu.VMEM((small_rows, width), BF16),
        pltpu.VMEM((small_rows, HEAD * HEADS), BF16),
        pltpu.VMEM((1, small_rows), jnp.int32),
        pltpu.VMEM((width, small_rows), BF16),
        pltpu.VMEM((HEAD * HEADS, small_rows), BF16),
        pltpu.VMEM((width, small_rows), BF16),
        pltpu.VMEM((small_rows, width), BF16),
        pltpu.VMEM((HEAD * HEADS, small_rows), BF16),
        pltpu.VMEM((1, HEAD * HEADS // 2), F32),
        pltpu.VMEM((1, HEAD * HEADS // 2), F32),
        pltpu.SemaphoreType.DMA((3,)),
    ]
    small_shape = jax.ShapeDtypeStruct((small_rows, width), BF16)
    sum_shapes = [jax.ShapeDtypeStruct((1, HEADS * HEAD // 2), F32)] * 2
    sent, small_out, *sums = call(
        first_kernel,
        [jax.ShapeDtypeStruct((HEADS, IN_ROWS, LANES), BF16), small_shape, *sum_shapes],
        [ANY] * 5,
        [ANY] * 4,
        (big_qkv, big_grad, small_qkv, small_grad, small_ids),
        [
            pltpu.VMEM((rows, width), BF16),
            pltpu.VMEM((rows, HEAD * HEADS), BF16),
            pltpu.VMEM((HEADS, IN_ROWS, LANES), BF16),
            pltpu.SemaphoreType.DMA((2, 2)),
            pltpu.SemaphoreType.DMA((2,)),
            *small_scratch,
        ],
        name="pack",
    )
    late_sums = summed(*sums, image, images, 1)
    sent, late_sums = lax.optimization_barrier((sent, late_sums))
    got = lax.all_to_all(sent, "seq", 0, 0, tiled=True)

    small_out, *sums = call(
        second_kernel,
        [small_shape, *sum_shapes],
        [ANY] * 4,
        [ANY] * 3,
        (small_qkv, small_grad, small_ids, small_out),
        small_scratch,
        flops=10**10,
        name="small",
        aliases={3: 0},
    )

    sums = late_sums + summed(*sums, image, images, 0)
    sums = jnp.pad(sums, (0, 3 * LANES - SHARE)).reshape(3, LANES)

    back = call(
        big_kernel,
        jax.ShapeDtypeStruct((parts, OUT_ROWS + SUM_ROWS, LANES), BF16),
        [VMEM, VMEM],
        VMEM,
        (got, sums),
        mebibytes=40,
        scratch=[pltpu.VMEM((4 * HEAD, length), BF16)],
        flops=10**10,
        name="big",
    )
    home = lax.all_to_all(back, "seq", 0, 0, tiled=True)

    extra = home[:, OUT_ROWS:].astype(F32)
    extra = extra[:, :4] + extra[:, 4:]
    share = jnp.sum(extra[:, :3], axis=0).reshape(3 * LANES)[:SHARE]
    quarters = [image // first % 2 * 2 + image // second % 2 for (_, first), (_, second) in STEPS]
    held = jnp.arange(4) == jnp.where(image % 2 == 0, *quarters)
    total = extra[:, 3, :HEAD].reshape(HEADS * HEAD) + jnp.where(held[:, None], share, 0.0).reshape(HEADS * HEAD)
    everyone = lax.all_to_all(
        jnp.broadcast_to(total, (images, 1, HEADS * HEAD)), "dp", 0, 0, tiled=True
    )
    bias_grad = jnp.sum(everyone, axis=(0, 1))

    big_out = call(
        unpack_kernel,
        jax.ShapeDtypeStruct((rows, width), BF16),
        [VMEM],
        VMEM,
        (home,),
        mebibytes=32,
        flops=10**9,
        name="unpack",
    )
    return big_out, small_out, bias_grad


def solution(mesh):
    spec = P(("dp", "seq"), None)
    return jax.shard_map(
        local,
        mesh=mesh,
        in_specs=(spec,) * 5,
        out_specs=(spec, spec, P()),
        check_vma=False,
    )
```

time: 110 us -> 104 us (0.945)
  Pallas kernels: 19.3 us -> 11.1 us
  starting transfers between devices: 39.1 us -> 42.4 us
    pallas_call x4, Pallas kernels: 19.3 us -> 11.1 us  [call(): pl.pallas_call(kernel, out_shape=shapes, in_specs=in_specs, out_specs=out...]
    ppermute x4, starting transfers between devices: 10.3 us -> 15.2 us  [the longest x2 8.77 us: summed(): sums = (kept + lax.ppermute(given, 'dp', pairs[0])).reshape(2 * SHARE)]
    all_to_all x1, waiting for transfers between devices: 20.6 us -> 17.3 us  [local(): home = lax.all_to_all(back, 'seq', 0, 0, tiled=True)]
    all_to_all x1, waiting for transfers between devices: 17.1 us -> 19.8 us  [local(): got = lax.all_to_all(sent, 'seq', 0, 0, tiled=True)]
    dynamic_slice x4 -> x2, local copies, waits for them, and re-layouts: 1.61 us -> 0.19 us  [summed(): given = lax.dynamic_slice(sums, ((1 - upper) * SHARE,), (SHARE,))]
    all_to_all x1, starting transfers between devices: 6.12 us -> 4.86 us  [local(): home = lax.all_to_all(back, 'seq', 0, 0, tiled=True)]
  transfers between devices with their start and end apart: 7 -> 7, of which waited for: 5 -> 5; matrix products, arithmetic and copies ran while one was open for 1% -> 0% of each run, Pallas kernels for 2% -> 1%
where the time goes in v3:
time: 104 us; the launch traced here: 103 us
  waiting for transfers between devices  45.9 us (44%)
  starting transfers between devices  42.4 us (41%)
  Pallas kernels  11.1 us (11%)
  local copies, waits for them, and re-layouts  1.79 us (2%)
    all_to_all x1, waiting for transfers between devices, local(): got = lax.all_to_all(sent, 'seq', 0, 0, tiled=True)  19.8 us
    all_to_all x1, waiting for transfers between devices, local(): home = lax.all_to_all(back, 'seq', 0, 0, tiled=True)  17.3 us
    all_to_all x1, starting transfers between devices, local(): got = lax.all_to_all(sent, 'seq', 0, 0, tiled=True)  15.2 us
    pallas_call x4, Pallas kernels, call(): pl.pallas_call(kernel, out_shape=shapes, in_specs=in_specs, out_specs=out...  11.1 us
    ppermute x2, starting transfers between devices, summed(): sums = (kept + lax.ppermute(given, 'dp', pairs[0])).reshape(2 * SHARE)  8.77 us
    all_to_all x1, starting transfers between devices, local(): lax.all_to_all(jnp.broadcast_to(total, (images, 1, HEADS * HEAD)), 'dp',...  7.2 us
    all_to_all x1, waiting for transfers between devices, local(): lax.all_to_all(jnp.broadcast_to(total, (images, 1, HEADS * HEAD)), 'dp',...  6.72 us
    ppermute x2, starting transfers between devices, summed(): sums = kept + lax.ppermute(given, 'dp', pairs[1])  6.4 us
  transfers between devices with their start and end apart: 7, of which 5 were waited for; matrix products, arithmetic and copies ran while one was open for 0% of the time, Pallas kernels for 1%

profile of v3, /device:TPU:1, one launch (start us, length us, event | category | flops | bytes accessed | tf_op | source)
XLA Modules:
  0.0 103.0 jit_solution(1186370468142504242)
XLA Ops:
  0.6 4.9 %pack.1 = (bf16[16,160,128]{2,1,0:T(8,128)(2,1)}, bf16[128,3840]{1,0:T(8,128)(2,1)}, f32[1,640]{1,0:T(1,128)}, f32[1,640]{1,0:T(1,128)}) custom-call(bf16[64,3840]{1,0:T(8,128)(2,1)} %qkv_hbm.1, bf16[64,1280]{1,0:T(8,128)(2,1)} %grad_hbm.1, bf16[128,3840]{1,0:T(8,128)(2,1)} %small_qkv.3, bf16[128,1280]{1,0:T(8,128)(2,1)} %small_grad.3, s32[1,128]{1,0:T(1,128)} %ids_hbm.3), custom_call_target="tpu_custom_call" | custom-call | bytes 1048576 | tf_op jit(solution)/shard_map/pack/pallas_call | solution.py:217
  5.5 8.1 %collective-permute-start = (f32[1,640]{1,0:T(1,128)}, f32[1,640]{1,0:T(1,128)S(1)}, u32[]{:S(2)}, u32[]{:S(2)}) collective-permute-start(f32[1,640]{1,0:T(1,128)} %get-tuple-element.14), channel_id=1, source_target_pairs={{16,336},{48,368},{80,272},{112,304},{144,464},{176,496},{208,400}... | collective-permute-start | bytes 7688 | tf_op jit(solution)/shard_map/ppermute | solution.py:237
  13.7 1.1 %collective-permute-done = f32[1,640]{1,0:T(1,128)S(1)} collective-permute-done((f32[1,640]{1,0:T(1,128)}, f32[1,640]{1,0:T(1,128)S(1)}, u32[]{:S(2)}, u32[]{:S(2)}) %collective-permute-start) | collective-permute-done | bytes 2592 | tf_op jit(solution)/shard_map/ppermute | solution.py:237
  14.8 0.1 dynamic-slice_reduce_fusion.2
  14.9 5.7 %collective-permute-start.1 = (f32[320]{0:T(512)S(1)}, f32[320]{0:T(512)S(1)}, u32[]{:S(2)}, u32[]{:S(2)}) collective-permute-start(f32[320]{0:T(512)S(1)} %get-tuple-element.23), channel_id=1, source_target_pairs={{16,304},{48,272},{80,368},{112,336},{144,432},{176,400},{208,496}... | collective-permute-start | bytes 3848 | tf_op jit(solution)/shard_map/ppermute | solution.py:241
  20.7 1.0 collective-permute-done.1
  21.7 15.2 %all-to-all-start = ((bf16[16,160,128]{2,1,0:T(8,128)(2,1)}), bf16[16,160,128]{2,1,0:T(8,128)(2,1)S(1)}, u32[]{:S(2)}, u32[]{:S(2)}) async-start(bf16[16,160,128]{2,1,0:T(8,128)(2,1)} %get-tuple-element.15), calls=%async_computation | async-start | bytes 1310720 | tf_op jit(solution)/shard_map/all_to_all | solution.py:287
  36.9 0.1 small.1
  37.0 0.7 collective-permute-start.2
  37.7 0.7 copy-done.1
  38.4 0.1 dynamic-slice_reduce_fusion
  38.4 0.7 collective-permute-start.3
  39.2 19.8 %all-to-all-done.in_ref = bf16[16,160,128]{2,1,0:T(8,128)(2,1)S(1)} async-done(((bf16[16,160,128]{2,1,0:T(8,128)(2,1)}), bf16[16,160,128]{2,1,0:T(8,128)(2,1)S(1)}, u32[]{:S(2)}, u32[]{:S(2)}) %all-to-all-start) | async-done | bytes 655392 | tf_op jit(solution)/shard_map/all_to_all | solution.py:287
  59.0 4.9 %big.1 = bf16[16,128,128]{2,1,0:T(8,128)(2,1)} custom-call(bf16[16,160,128]{2,1,0:T(8,128)(2,1)S(1)} %all-to-all-done.in_ref, f32[3,128]{1,0:T(4,128)S(1)} %pad_bitcast_fusion.sums_ref), custom_call_target="tpu_custom_call" | custom-call | flops 10000000000 | bytes 1048576 | tf_op jit(solution)/shard_map/big/pallas_call | solution.py:217
  63.9 4.9 %all-to-all-start.1 = ((bf16[16,128,128]{2,1,0:T(8,128)(2,1)}), bf16[16,128,128]{2,1,0:T(8,128)(2,1)S(1)}, u32[]{:S(2)}, u32[]{:S(2)}) async-start(bf16[16,128,128]{2,1,0:T(8,128)(2,1)} %big.1), calls=%async_computation.1 | async-start | bytes 1048576 | tf_op jit(solution)/shard_map/all_to_all | solution.py:315
  68.8 17.3 %all-to-all-done.1.in_ref = bf16[16,128,128]{2,1,0:T(8,128)(2,1)S(1)} async-done(((bf16[16,128,128]{2,1,0:T(8,128)(2,1)}), bf16[16,128,128]{2,1,0:T(8,128)(2,1)S(1)}, u32[]{:S(2)}, u32[]{:S(2)}) %all-to-all-start.1) | async-done | bytes 524320 | tf_op jit(solution)/shard_map/all_to_all | solution.py:315
  86.2 0.1 reshape_squeeze.3
  86.3 0.1 broadcast_select_fusion
  86.3 0.1 select_n.90
  86.4 0.7 broadcast_in_dim.29
  87.2 7.2 %all-to-all-start.2 = ((f32[32,1,1280]{2,1,0:T(1,128)}), f32[32,1,1280]{2,1,0:T(1,128)S(1)}, u32[]{:S(2)}, u32[]{:S(2)}) async-start(f32[32,1,1280]{2,1,0:T(1,128)} %broadcast_in_dim.29), calls=%async_computation.2 | async-start | bytes 327680 | tf_op jit(solution)/shard_map/all_to_all | solution.py:323
  94.4 1.2 %unpack.1 = bf16[64,3840]{1,0:T(8,128)(2,1)} custom-call(bf16[16,128,128]{2,1,0:T(8,128)(2,1)S(1)} %all-to-all-done.1.in_ref), custom_call_target="tpu_custom_call" | custom-call | flops 1000000000 | bytes 1048576 | tf_op jit(solution)/shard_map/unpack/pallas_call | solution.py:217
  95.6 6.7 %all-to-all-done.2 = f32[32,1,1280]{2,1,0:T(1,128)S(1)} async-done(((f32[32,1,1280]{2,1,0:T(1,128)}), f32[32,1,1280]{2,1,0:T(1,128)S(1)}, u32[]{:S(2)}, u32[]{:S(2)}) %all-to-all-start.2) | async-done | bytes 163872 | tf_op jit(solution)/shard_map/all_to_all | solution.py:323
  102.3 0.7 reduce_sum.19
  (16 shorter events, 0.1 us)
Async XLA Ops:
  5.5 9.3 %collective-permute-start = (f32[1,640]{1,0:T(1,128)}, f32[1,640]{1,0:T(1,128)S(1)}, u32[]{:S(2)}, u32[]{:S(2)}) collective-permute-start(f32[1,640]{1,0:T(1,128)} %get-tuple-element.14), channel_id=1, source_target_pairs={{16,336},{48,368},{80,272},{112,304},{144,464},{176,496},{208,400}... | collective-permute-start | bytes 7688 | tf_op jit(solution)/shard_map/ppermute | solution.py:237
  13.7 1.1 %copy-start = (f32[1,640]{1,0:T(1,128)S(1)}, f32[1,640]{1,0:T(1,128)}, u32[]{:S(2)}) copy-start(f32[1,640]{1,0:T(1,128)} %get-tuple-element.13) | copy-start | bytes 7684
  14.9 6.7 %collective-permute-start.1 = (f32[320]{0:T(512)S(1)}, f32[320]{0:T(512)S(1)}, u32[]{:S(2)}, u32[]{:S(2)}) collective-permute-start(f32[320]{0:T(512)S(1)} %get-tuple-element.23), channel_id=1, source_target_pairs={{16,304},{48,272},{80,368},{112,336},{144,432},{176,400},{208,496}... | collective-permute-start | bytes 3848 | tf_op jit(solution)/shard_map/ppermute | solution.py:241
  21.7 37.3 %all-to-all-start = ((bf16[16,160,128]{2,1,0:T(8,128)(2,1)}), bf16[16,160,128]{2,1,0:T(8,128)(2,1)S(1)}, u32[]{:S(2)}, u32[]{:S(2)}) async-start(bf16[16,160,128]{2,1,0:T(8,128)(2,1)} %get-tuple-element.15), calls=%async_computation | async-start | bytes 1310720 | tf_op jit(solution)/shard_map/all_to_all | solution.py:287
  37.0 0.7 collective-permute-start.2
  37.7 0.7 copy-start.1
  38.4 0.7 collective-permute-start.3
  63.9 22.2 %all-to-all-start.1 = ((bf16[16,128,128]{2,1,0:T(8,128)(2,1)}), bf16[16,128,128]{2,1,0:T(8,128)(2,1)S(1)}, u32[]{:S(2)}, u32[]{:S(2)}) async-start(bf16[16,128,128]{2,1,0:T(8,128)(2,1)} %big.1), calls=%async_computation.1 | async-start | bytes 1048576 | tf_op jit(solution)/shard_map/all_to_all | solution.py:315
  87.2 15.2 %all-to-all-start.2 = ((f32[32,1,1280]{2,1,0:T(1,128)}), f32[32,1,1280]{2,1,0:T(1,128)S(1)}, u32[]{:S(2)}, u32[]{:S(2)}) async-start(f32[32,1,1280]{2,1,0:T(1,128)} %broadcast_in_dim.29), calls=%async_computation.2 | async-start | bytes 327680 | tf_op jit(solution)/shard_map/all_to_all | solution.py:323

commit v4 on v3

--- a/solution.py
+++ b/solution.py
@@ -11,10 +11,11 @@
 HEADS = 16
 SCALE = HEAD ** (-0.5)
 LANES = 128
+TOGETHER = 1
 IN_ROWS = 2 * HEAD
 OUT_ROWS = 3 * HEAD // 2
 SUM_ROWS = 8
-STEPS = (((2, 2), (4, 4)), ((20, 4), (18, 2)))
+STEPS = (((2, 2), (4, 4)), ((20, 4), (2, 2)))
 SHARE = HEADS * HEAD // 4
 EXPONENT = SCALE * math.log2(math.e)
 F32 = jnp.float32
@@ -45,7 +46,7 @@
     return [pltpu.make_async_copy(sources[at], scratch[at], sems.at[at]) for at in range(3)]
 
 
-def small_images(loads, out_hbm, kept_hbm, given_hbm, core, scratch):
+def small_images(loads, out_hbm, kept_hbm, given_hbm, core, together, scratch):
     qkv, grads, ids_ref, qkv_t, grad_t, out_t, out, query_t, kept, given, sems = scratch
     rows = qkv.shape[0]
     for load in loads:
@@ -55,26 +56,32 @@
     qkv_t[...] = qkv[...].T
     grad_t[...] = grads[...].T
 
-    def part(head, which):
-        first = 3 * HEAD * head + HEAD * which
-        return qkv_t[first : first + HEAD]
-
-    def grad(head):
-        return grad_t[HEAD * head : HEAD * (head + 1)]
-
-    heads = range(HEADS)
-    scores = [jnp.where(allowed, dot(part(head, 1), part(head, 0), 0, 0), -1e30) for head in heads]
-    upstream = [dot(part(head, 2), grad(head), 0, 0) for head in heads]
-    both = [slopes_of(*pair) for pair in zip(scores, upstream)]
-    query_grad = [(dot(part(head, 1), both[head][1], 1, 0) * SCALE).astype(BF16) for head in heads]
-    key_grad = [(dot(part(head, 0), both[head][1], 1, 1) * SCALE).astype(BF16) for head in heads]
-    value_grad = [dot(grad(head), both[head][0], 1, 1).astype(BF16) for head in heads]
-    for head in heads:
-        first = 3 * HEAD * head
-        out_t[first : first + HEAD] = query_grad[head]
-        query_t[HEAD * head : HEAD * (head + 1)] = query_grad[head]
-        out_t[first + HEAD : first + 2 * HEAD] = key_grad[head]
-        out_t[first + 2 * HEAD : first + 3 * HEAD] = value_grad[head]
+    def place(head, which=0, count=3):
+        first = count * HEAD * head + HEAD * which
+        return pl.ds(first if isinstance(first, int) else pl.multiple_of(first, 16), HEAD)
+
+    def some(heads):
+        query, key, value = ([qkv_t[place(head, which)] for head in heads] for which in range(3))
+        grad = [grad_t[place(head, 0, 1)] for head in heads]
+        scores = [jnp.where(allowed, dot(*pair, 0, 0), -1e30) for pair in zip(key, query)]
+        upstream = [dot(*pair, 0, 0) for pair in zip(value, grad)]
+        weights, slopes = zip(*[slopes_of(*pair) for pair in zip(scores, upstream)])
+        query_grad = [(dot(*pair, 1, 0) * SCALE).astype(BF16) for pair in zip(key, slopes)]
+        key_grad = [(dot(*pair, 1, 1) * SCALE).astype(BF16) for pair in zip(query, slopes)]
+        value_grad = [dot(*pair, 1, 1).astype(BF16) for pair in zip(grad, weights)]
+        for at, head in enumerate(heads):
+            query_t[place(head, 0, 1)] = query_grad[at]
+            for which, result in enumerate((query_grad, key_grad, value_grad)):
+                out_t[place(head, which)] = result[at]
+
+    if together == HEADS:
+        some(range(HEADS))
+    else:
+
+        @pl.loop(0, HEADS // together)
+        def _(step):
+            some([step * together + at for at in range(together)])
+
     sums = dot(jnp.ones((8, rows), BF16), query_t[...], 1, 1)[:1]
     half = HEADS * HEAD // 2
     upper = lax.axis_index("dp") // STEPS[core][0][1] % 2
@@ -155,21 +162,21 @@
 
     @pl.when(late)
     def _():
-        small_images(after, small_out, kept_hbm, given_hbm, 1, scratch)
+        small_images(after, small_out, kept_hbm, given_hbm, 1, TOGETHER, scratch)
 
     for store in stores:
         store.wait()
 
 
 def second_kernel(
-    small_qkv, small_grad, ids_hbm, before, small_out, kept_hbm, given_hbm, *scratch
+    small_qkv, small_grad, ids_hbm, before, kept_before, given_before, small_out, kept_hbm, given_hbm, *scratch
 ):
     @pl.when(lax.axis_index("dp") % 2 == 0)
     def _():
         loads = small_loads(small_qkv, small_grad, ids_hbm, scratch)
         for load in loads:
             load.start()
-        small_images(loads, small_out, kept_hbm, given_hbm, 0, scratch)
+        small_images(loads, small_out, kept_hbm, given_hbm, 0, HEADS, scratch)
 
 
 def pieces(row):
@@ -231,15 +238,9 @@
 ANY = pl.BlockSpec(memory_space=pl.ANY)
 
 
-def summed(kept, given, image, images, core):
-    (first, _), (second, bit) = STEPS[core]
-    pairs = [[(at, at ^ step) for at in range(images) if at % 2 == core] for step in (first, second)]
-    sums = (kept + lax.ppermute(given, "dp", pairs[0])).reshape(2 * SHARE)
-    upper = image // bit % 2
-    kept = lax.dynamic_slice(sums, (upper * SHARE,), (SHARE,))
-    given = lax.dynamic_slice(sums, ((1 - upper) * SHARE,), (SHARE,))
-    sums = kept + lax.ppermute(given, "dp", pairs[1])
-    return jnp.where(image % 2 == core, sums, 0.0)
+def halved(given, images, step, cores):
+    pairs = [(at, at ^ STEPS[at % 2][step][0]) for at in range(images) if at % 2 in cores]
+    return lax.ppermute(given, "dp", pairs)
 
 
 def local(big_qkv, big_grad, small_qkv, small_grad, small_ids):
@@ -282,23 +283,28 @@
         ],
         name="pack",
     )
-    late_sums = summed(*sums, image, images, 1)
-    sent, late_sums = lax.optimization_barrier((sent, late_sums))
+    late = halved(sums[1], images, 0, (1,))
+    sent, late = lax.optimization_barrier((sent, late))
     got = lax.all_to_all(sent, "seq", 0, 0, tiled=True)
 
     small_out, *sums = call(
         second_kernel,
         [small_shape, *sum_shapes],
-        [ANY] * 4,
+        [ANY] * 6,
         [ANY] * 3,
-        (small_qkv, small_grad, small_ids, small_out),
+        (small_qkv, small_grad, small_ids, small_out, *sums),
         small_scratch,
         flops=10**10,
         name="small",
-        aliases={3: 0},
-    )
-
-    sums = late_sums + summed(*sums, image, images, 0)
+        aliases={3: 0, 4: 1, 5: 2},
+    )
+
+    early = halved(sums[1], images, 0, (0,))
+    sums = (sums[0] + late + early).reshape(2 * SHARE)
+    upper = jnp.where(image % 2 == 0, *[image // STEPS[core][1][1] % 2 for core in range(2)])
+    kept = lax.dynamic_slice(sums, (upper * SHARE,), (SHARE,))
+    given = lax.dynamic_slice(sums, ((1 - upper) * SHARE,), (SHARE,))
+    sums = kept + halved(given, images, 1, (0, 1))
     sums = jnp.pad(sums, (0, 3 * LANES - SHARE)).reshape(3, LANES)
 
     back = call(

time: 104 us -> 103 us (level)
  Pallas kernels: 11.1 us -> 16.7 us
  waiting for transfers between devices: 45.9 us -> 42.2 us
  starting transfers between devices: 42.4 us -> 39.4 us
    pallas_call x4, Pallas kernels: 11.1 us -> 16.7 us  [call(): pl.pallas_call(kernel, out_shape=shapes, in_specs=in_specs, out_specs=out...]
    all_to_all x1, waiting for transfers between devices: 19.8 us -> 16.1 us  [local(): got = lax.all_to_all(sent, 'seq', 0, 0, tiled=True)]
    ppermute x4 -> x3, starting transfers between devices: 15.2 us -> 12.2 us  [halved(): return lax.ppermute(given, 'dp', pairs)]
    ppermute x4 -> x3, waiting for transfers between devices: 2.1 us -> 2.14 us  [halved(): return lax.ppermute(given, 'dp', pairs)]
  transfers between devices with their start and end apart: 7 -> 6, of which waited for: 5 -> 5; matrix products, arithmetic and copies ran while one was open for 0% -> 0% of each run, Pallas kernels for 1% -> 1%
where the time goes in v4:
time: 103 us; the launch traced here: 102 us
  waiting for transfers between devices  42.2 us (41%)
  starting transfers between devices  39.4 us (38%)
  Pallas kernels  16.7 us (16%)
  local copies, waits for them, and re-layouts  1.69 us (2%)
    all_to_all x1, waiting for transfers between devices, local(): home = lax.all_to_all(back, 'seq', 0, 0, tiled=True)  17.3 us
    pallas_call x4, Pallas kernels, call(): pl.pallas_call(kernel, out_shape=shapes, in_specs=in_specs, out_specs=out...  16.7 us
    all_to_all x1, waiting for transfers between devices, local(): got = lax.all_to_all(sent, 'seq', 0, 0, tiled=True)  16.1 us
    all_to_all x1, starting transfers between devices, local(): got = lax.all_to_all(sent, 'seq', 0, 0, tiled=True)  14.9 us
    ppermute x3, starting transfers between devices, halved(): return lax.ppermute(given, 'dp', pairs)  12.2 us
    all_to_all x1, starting transfers between devices, local(): lax.all_to_all(jnp.broadcast_to(total, (images, 1, HEADS * HEAD)), 'dp',...  7.44 us
    all_to_all x1, waiting for transfers between devices, local(): lax.all_to_all(jnp.broadcast_to(total, (images, 1, HEADS * HEAD)), 'dp',...  6.72 us
    all_to_all x1, starting transfers between devices, local(): home = lax.all_to_all(back, 'seq', 0, 0, tiled=True)  4.87 us
  transfers between devices with their start and end apart: 6, of which 5 were waited for; matrix products, arithmetic and copies ran while one was open for 0% of the time, Pallas kernels for 1%

profile of v4, /device:TPU:1, one launch (start us, length us, event | category | flops | bytes accessed | tf_op | source)
XLA Modules:
  0.0 101.8 jit_solution(4922613849093113800)
XLA Ops:
  0.6 10.5 %pack.1 = (bf16[16,160,128]{2,1,0:T(8,128)(2,1)}, bf16[128,3840]{1,0:T(8,128)(2,1)}, f32[1,640]{1,0:T(1,128)}, f32[1,640]{1,0:T(1,128)}) custom-call(bf16[64,3840]{1,0:T(8,128)(2,1)} %qkv_hbm.1, bf16[64,1280]{1,0:T(8,128)(2,1)} %grad_hbm.1, bf16[128,3840]{1,0:T(8,128)(2,1)} %small_qkv.3, bf16[128,1280]{1,0:T(8,128)(2,1)} %small_grad.3, s32[1,128]{1,0:T(1,128)} %ids_hbm.3), custom_call_target="tpu_custom_call" | custom-call | bytes 1048576 | tf_op jit(solution)/shard_map/pack/pallas_call | solution.py:224
  11.2 8.1 %collective-permute-start = (f32[1,640]{1,0:T(1,128)}, f32[1,640]{1,0:T(1,128)S(1)}, u32[]{:S(2)}, u32[]{:S(2)}) collective-permute-start(f32[1,640]{1,0:T(1,128)} %get-tuple-element.13.given_before), channel_id=1, source_target_pairs={{16,336},{48,368},{80,272},{112,304},{144,464},{176,496},{208,400}... | collective-permute-start | bytes 7688 | tf_op jit(solution)/shard_map/ppermute | solution.py:243
  19.3 1.2 %collective-permute-done = f32[1,640]{1,0:T(1,128)S(1)} collective-permute-done((f32[1,640]{1,0:T(1,128)}, f32[1,640]{1,0:T(1,128)S(1)}, u32[]{:S(2)}, u32[]{:S(2)}) %collective-permute-start) | collective-permute-done | bytes 2592 | tf_op jit(solution)/shard_map/ppermute | solution.py:243
  20.4 14.9 %all-to-all-start = ((bf16[16,160,128]{2,1,0:T(8,128)(2,1)}), bf16[16,160,128]{2,1,0:T(8,128)(2,1)S(1)}, u32[]{:S(2)}, u32[]{:S(2)}) async-start(bf16[16,160,128]{2,1,0:T(8,128)(2,1)} %get-tuple-element.14), calls=%async_computation | async-start | bytes 1310720 | tf_op jit(solution)/shard_map/all_to_all | solution.py:288
  35.4 0.1 small.1
  35.4 0.7 collective-permute-start.1
  36.2 0.0 copy-start
  36.2 0.0 collective-permute-done.1
  36.2 0.7 copy-done
  36.9 0.1 dynamic-slice_reduce_fusion
  37.0 3.4 %collective-permute-start.2 = (f32[320]{0:T(512)S(1)}, f32[320]{0:T(512)S(1)}, u32[]{:S(2)}, u32[]{:S(2)}) collective-permute-start(f32[320]{0:T(512)S(1)} %get-tuple-element.21), channel_id=1, source_target_pairs={{0,64},{16,48},{32,96},{48,16},{64,0},{80,112},{96,32},{112,80},{1... | collective-permute-start | bytes 3848 | tf_op jit(solution)/shard_map/ppermute | solution.py:243
  40.4 1.0 collective-permute-done.2
  41.4 16.1 %all-to-all-done.in_ref = bf16[16,160,128]{2,1,0:T(8,128)(2,1)S(1)} async-done(((bf16[16,160,128]{2,1,0:T(8,128)(2,1)}), bf16[16,160,128]{2,1,0:T(8,128)(2,1)S(1)}, u32[]{:S(2)}, u32[]{:S(2)}) %all-to-all-start) | async-done | bytes 655392 | tf_op jit(solution)/shard_map/all_to_all | solution.py:288
  57.5 4.9 %big.1 = bf16[16,128,128]{2,1,0:T(8,128)(2,1)} custom-call(bf16[16,160,128]{2,1,0:T(8,128)(2,1)S(1)} %all-to-all-done.in_ref, f32[3,128]{1,0:T(4,128)S(1)} %pad_bitcast_fusion.sums_ref), custom_call_target="tpu_custom_call" | custom-call | flops 10000000000 | bytes 1048576 | tf_op jit(solution)/shard_map/big/pallas_call | solution.py:224
  62.4 4.9 %all-to-all-start.1 = ((bf16[16,128,128]{2,1,0:T(8,128)(2,1)}), bf16[16,128,128]{2,1,0:T(8,128)(2,1)S(1)}, u32[]{:S(2)}, u32[]{:S(2)}) async-start(bf16[16,128,128]{2,1,0:T(8,128)(2,1)} %big.1), calls=%async_computation.1 | async-start | bytes 1048576 | tf_op jit(solution)/shard_map/all_to_all | solution.py:321
  67.3 17.3 %all-to-all-done.1.in_ref = bf16[16,128,128]{2,1,0:T(8,128)(2,1)S(1)} async-done(((bf16[16,128,128]{2,1,0:T(8,128)(2,1)}), bf16[16,128,128]{2,1,0:T(8,128)(2,1)S(1)}, u32[]{:S(2)}, u32[]{:S(2)}) %all-to-all-start.1) | async-done | bytes 524320 | tf_op jit(solution)/shard_map/all_to_all | solution.py:321
  84.7 0.1 reshape_squeeze.3
  84.8 0.1 broadcast_select_fusion
  84.8 0.1 select_n.66
  84.9 0.7 broadcast_in_dim.23
  85.7 7.4 %all-to-all-start.2 = ((f32[32,1,1280]{2,1,0:T(1,128)}), f32[32,1,1280]{2,1,0:T(1,128)S(1)}, u32[]{:S(2)}, u32[]{:S(2)}) async-start(f32[32,1,1280]{2,1,0:T(1,128)} %broadcast_in_dim.23), calls=%async_computation.2 | async-start | bytes 327680 | tf_op jit(solution)/shard_map/all_to_all | solution.py:329
  93.1 1.2 %unpack.1 = bf16[64,3840]{1,0:T(8,128)(2,1)} custom-call(bf16[16,128,128]{2,1,0:T(8,128)(2,1)S(1)} %all-to-all-done.1.in_ref), custom_call_target="tpu_custom_call" | custom-call | flops 1000000000 | bytes 1048576 | tf_op jit(solution)/shard_map/unpack/pallas_call | solution.py:224
  94.3 6.7 %all-to-all-done.2 = f32[32,1,1280]{2,1,0:T(1,128)S(1)} async-done(((f32[32,1,1280]{2,1,0:T(1,128)}), f32[32,1,1280]{2,1,0:T(1,128)S(1)}, u32[]{:S(2)}, u32[]{:S(2)}) %all-to-all-start.2) | async-done | bytes 163872 | tf_op jit(solution)/shard_map/all_to_all | solution.py:329
  101.1 0.7 reduce_sum.19
  (9 shorter events, 0.1 us)
Async XLA Ops:
  11.2 9.3 %collective-permute-start = (f32[1,640]{1,0:T(1,128)}, f32[1,640]{1,0:T(1,128)S(1)}, u32[]{:S(2)}, u32[]{:S(2)}) collective-permute-start(f32[1,640]{1,0:T(1,128)} %get-tuple-element.13.given_before), channel_id=1, source_target_pairs={{16,336},{48,368},{80,272},{112,304},{144,464},{176,496},{208,400}... | collective-permute-start | bytes 7688 | tf_op jit(solution)/shard_map/ppermute | solution.py:243
  20.4 37.0 %all-to-all-start = ((bf16[16,160,128]{2,1,0:T(8,128)(2,1)}), bf16[16,160,128]{2,1,0:T(8,128)(2,1)S(1)}, u32[]{:S(2)}, u32[]{:S(2)}) async-start(bf16[16,160,128]{2,1,0:T(8,128)(2,1)} %get-tuple-element.14), calls=%async_computation | async-start | bytes 1310720 | tf_op jit(solution)/shard_map/all_to_all | solution.py:288
  35.4 0.8 collective-permute-start.1
  36.2 0.7 copy-start
  37.0 4.4 %collective-permute-start.2 = (f32[320]{0:T(512)S(1)}, f32[320]{0:T(512)S(1)}, u32[]{:S(2)}, u32[]{:S(2)}) collective-permute-start(f32[320]{0:T(512)S(1)} %get-tuple-element.21), channel_id=1, source_target_pairs={{0,64},{16,48},{32,96},{48,16},{64,0},{80,112},{96,32},{112,80},{1... | collective-permute-start | bytes 3848 | tf_op jit(solution)/shard_map/ppermute | solution.py:243
  62.4 22.2 %all-to-all-start.1 = ((bf16[16,128,128]{2,1,0:T(8,128)(2,1)}), bf16[16,128,128]{2,1,0:T(8,128)(2,1)S(1)}, u32[]{:S(2)}, u32[]{:S(2)}) async-start(bf16[16,128,128]{2,1,0:T(8,128)(2,1)} %big.1), calls=%async_computation.1 | async-start | bytes 1048576 | tf_op jit(solution)/shard_map/all_to_all | solution.py:321
  85.7 15.4 %all-to-all-start.2 = ((f32[32,1,1280]{2,1,0:T(1,128)}), f32[32,1,1280]{2,1,0:T(1,128)S(1)}, u32[]{:S(2)}, u32[]{:S(2)}) async-start(f32[32,1,1280]{2,1,0:T(1,128)} %broadcast_in_dim.23), calls=%async_computation.2 | async-start | bytes 327680 | tf_op jit(solution)/shard_map/all_to_all | solution.py:329

commit v5 on v4

--- a/solution.py
+++ b/solution.py
@@ -11,6 +11,8 @@
 HEADS = 16
 SCALE = HEAD ** (-0.5)
 LANES = 128
+FIRST_PART = 10
+FIRST_IMAGE = 21
 TOGETHER = 1
 IN_ROWS = 2 * HEAD
 OUT_ROWS = 3 * HEAD // 2
@@ -249,6 +251,8 @@
     images = lax.axis_size("dp")
     parts = lax.axis_size("seq")
     length = rows * parts
+    ring = [[(at + FIRST_PART) % parts for at in range(parts)]]
+    plane = [[(at + FIRST_IMAGE) % images for at in range(images)]]
     width = 3 * HEAD * HEADS
     image = lax.axis_index("dp")
 
@@ -285,7 +289,7 @@
     )
     late = halved(sums[1], images, 0, (1,))
     sent, late = lax.optimization_barrier((sent, late))
-    got = lax.all_to_all(sent, "seq", 0, 0, tiled=True)
+    got = lax.all_to_all(sent, "seq", 0, 0, axis_index_groups=ring, tiled=True)
 
     small_out, *sums = call(
         second_kernel,
@@ -318,7 +322,7 @@
         flops=10**10,
         name="big",
     )
-    home = lax.all_to_all(back, "seq", 0, 0, tiled=True)
+    home = lax.all_to_all(back, "seq", 0, 0, axis_index_groups=ring, tiled=True)
 
     extra = home[:, OUT_ROWS:].astype(F32)
     extra = extra[:, :4] + extra[:, 4:]
@@ -327,7 +331,7 @@
     held = jnp.arange(4) == jnp.where(image % 2 == 0, *quarters)
     total = extra[:, 3, :HEAD].reshape(HEADS * HEAD) + jnp.where(held[:, None], share, 0.0).reshape(HEADS * HEAD)
     everyone = lax.all_to_all(
-        jnp.broadcast_to(total, (images, 1, HEADS * HEAD)), "dp", 0, 0, tiled=True
+        jnp.broadcast_to(total, (images, 1, HEADS * HEAD)), "dp", 0, 0, axis_index_groups=plane, tiled=True
     )
     bias_grad = jnp.sum(everyone, axis=(0, 1))
 
@@ -337,7 +341,7 @@
         [VMEM],
         VMEM,
         (home,),
-        mebibytes=32,
+        mebibytes=8,
         flops=10**9,
         name="unpack",
     )

time: 103 us -> 97.7 us (0.949)
  waiting for transfers between devices: 42.2 us -> 27.4 us
  starting transfers between devices: 39.4 us -> 49.7 us
    all_to_all x2, waiting for transfers between devices: 33.4 us -> 23.2 us  [the longest x1 13.2 us: local(): home = lax.all_to_all(back, 'seq', 0, 0, axis_index_groups=ring, tiled=True)]
    all_to_all x2, starting transfers between devices: 19.8 us -> 27.9 us  [the longest x1 16.8 us: local(): got = lax.all_to_all(sent, 'seq', 0, 0, axis_index_groups=ring, tiled=True)]
    all_to_all x1, waiting for transfers between devices: 6.72 us -> 1.83 us  [local(): lax.all_to_all(jnp.broadcast_to(total, (images, 1, HEADS * HEAD)), 'dp',...]
    all_to_all x1, starting transfers between devices: 7.44 us -> 9.96 us  [local(): lax.all_to_all(jnp.broadcast_to(total, (images, 1, HEADS * HEAD)), 'dp',...]
where the time goes in v5:
time: 97.7 us; the launch traced here: 97.2 us
  starting transfers between devices  49.7 us (51%)
  waiting for transfers between devices  27.4 us (28%)
  Pallas kernels  16.7 us (17%)
  local copies, waits for them, and re-layouts  1.69 us (2%)
    all_to_all x1, starting transfers between devices, local(): got = lax.all_to_all(sent, 'seq', 0, 0, axis_index_groups=ring, tiled=True)  16.8 us
    pallas_call x4, Pallas kernels, call(): pl.pallas_call(kernel, out_shape=shapes, in_specs=in_specs, out_specs=out...  16.7 us
    all_to_all x1, waiting for transfers between devices, local(): home = lax.all_to_all(back, 'seq', 0, 0, axis_index_groups=ring, tiled=True)  13.2 us
    ppermute x3, starting transfers between devices, halved(): return lax.ppermute(given, 'dp', pairs)  11.9 us
    all_to_all x1, starting transfers between devices, local(): home = lax.all_to_all(back, 'seq', 0, 0, axis_index_groups=ring, tiled=True)  11.1 us
    all_to_all x1, waiting for transfers between devices, local(): got = lax.all_to_all(sent, 'seq', 0, 0, axis_index_groups=ring, tiled=True)  9.97 us
    all_to_all x1, starting transfers between devices, local(): lax.all_to_all(jnp.broadcast_to(total, (images, 1, HEADS * HEAD)), 'dp',...  9.96 us
    ppermute x3, waiting for transfers between devices, halved(): return lax.ppermute(given, 'dp', pairs)  2.39 us
  transfers between devices with their start and end apart: 6, of which 5 were waited for; matrix products, arithmetic and copies ran while one was open for 0% of the time, Pallas kernels for 1%

profile of v5, /device:TPU:1, one launch (start us, length us, event | category | flops | bytes accessed | tf_op | source)
XLA Modules:
  0.0 97.2 jit_solution(17655358260147461836)
XLA Ops:
  0.6 10.5 %pack.1 = (bf16[16,160,128]{2,1,0:T(8,128)(2,1)}, bf16[128,3840]{1,0:T(8,128)(2,1)}, f32[1,640]{1,0:T(1,128)}, f32[1,640]{1,0:T(1,128)}) custom-call(bf16[64,3840]{1,0:T(8,128)(2,1)} %qkv_hbm.1, bf16[64,1280]{1,0:T(8,128)(2,1)} %grad_hbm.1, bf16[128,3840]{1,0:T(8,128)(2,1)} %small_qkv.3, bf16[128,1280]{1,0:T(8,128)(2,1)} %small_grad.3, s32[1,128]{1,0:T(1,128)} %ids_hbm.3), custom_call_target="tpu_custom_call" | custom-call | bytes 1048576 | tf_op jit(solution)/shard_map/pack/pallas_call | solution.py:226
  11.2 8.1 %collective-permute-start = (f32[1,640]{1,0:T(1,128)}, f32[1,640]{1,0:T(1,128)S(1)}, u32[]{:S(2)}, u32[]{:S(2)}) collective-permute-start(f32[1,640]{1,0:T(1,128)} %get-tuple-element.13.given_before), channel_id=1, source_target_pairs={{16,336},{48,368},{80,272},{112,304},{144,464},{176,496},{208,400}... | collective-permute-start | bytes 7688 | tf_op jit(solution)/shard_map/ppermute | solution.py:245
  19.3 1.2 %collective-permute-done = f32[1,640]{1,0:T(1,128)S(1)} collective-permute-done((f32[1,640]{1,0:T(1,128)}, f32[1,640]{1,0:T(1,128)S(1)}, u32[]{:S(2)}, u32[]{:S(2)}) %collective-permute-start) | collective-permute-done | bytes 2592 | tf_op jit(solution)/shard_map/ppermute | solution.py:245
  20.4 16.8 %all-to-all-start = ((bf16[16,160,128]{2,1,0:T(8,128)(2,1)}), bf16[16,160,128]{2,1,0:T(8,128)(2,1)S(1)}, u32[]{:S(2)}, u32[]{:S(2)}) async-start(bf16[16,160,128]{2,1,0:T(8,128)(2,1)} %get-tuple-element.14), calls=%async_computation | async-start | bytes 1310720 | tf_op jit(solution)/shard_map/all_to_all | solution.py:292
  37.3 0.7 collective-permute-start.1
  38.0 0.0 copy-start
  38.0 0.0 collective-permute-done.1
  38.0 0.7 copy-done
  38.7 0.1 dynamic-slice_reduce_fusion
  38.8 3.1 %collective-permute-start.2 = (f32[320]{0:T(512)S(1)}, f32[320]{0:T(512)S(1)}, u32[]{:S(2)}, u32[]{:S(2)}) collective-permute-start(f32[320]{0:T(512)S(1)} %get-tuple-element.21), channel_id=1, source_target_pairs={{0,64},{16,48},{32,96},{48,16},{64,0},{80,112},{96,32},{112,80},{1... | collective-permute-start | bytes 3848 | tf_op jit(solution)/shard_map/ppermute | solution.py:245
  41.9 1.2 %collective-permute-done.2 = f32[320]{0:T(512)S(1)} collective-permute-done((f32[320]{0:T(512)S(1)}, f32[320]{0:T(512)S(1)}, u32[]{:S(2)}, u32[]{:S(2)}) %collective-permute-start.2) | collective-permute-done | bytes 1312 | tf_op jit(solution)/shard_map/ppermute | solution.py:245
  43.1 10.0 %all-to-all-done.in_ref = bf16[16,160,128]{2,1,0:T(8,128)(2,1)S(1)} async-done(((bf16[16,160,128]{2,1,0:T(8,128)(2,1)}), bf16[16,160,128]{2,1,0:T(8,128)(2,1)S(1)}, u32[]{:S(2)}, u32[]{:S(2)}) %all-to-all-start) | async-done | bytes 655392 | tf_op jit(solution)/shard_map/all_to_all | solution.py:292
  53.1 4.9 %big.1 = bf16[16,128,128]{2,1,0:T(8,128)(2,1)} custom-call(bf16[16,160,128]{2,1,0:T(8,128)(2,1)S(1)} %all-to-all-done.in_ref, f32[3,128]{1,0:T(4,128)S(1)} %pad_bitcast_fusion.sums_ref), custom_call_target="tpu_custom_call" | custom-call | flops 10000000000 | bytes 1048576 | tf_op jit(solution)/shard_map/big/pallas_call | solution.py:226
  58.1 11.1 %all-to-all-start.1 = ((bf16[16,128,128]{2,1,0:T(8,128)(2,1)}), bf16[16,128,128]{2,1,0:T(8,128)(2,1)S(1)}, u32[]{:S(2)}, u32[]{:S(2)}) async-start(bf16[16,128,128]{2,1,0:T(8,128)(2,1)} %big.1), calls=%async_computation.1 | async-start | bytes 1048576 | tf_op jit(solution)/shard_map/all_to_all | solution.py:325
  69.1 13.2 %all-to-all-done.1.in_ref = bf16[16,128,128]{2,1,0:T(8,128)(2,1)S(1)} async-done(((bf16[16,128,128]{2,1,0:T(8,128)(2,1)}), bf16[16,128,128]{2,1,0:T(8,128)(2,1)S(1)}, u32[]{:S(2)}, u32[]{:S(2)}) %all-to-all-start.1) | async-done | bytes 524320 | tf_op jit(solution)/shard_map/all_to_all | solution.py:325
  82.5 0.1 reshape_squeeze.3
  82.5 0.1 broadcast_select_fusion
  82.6 0.1 select_n.66
  82.7 0.7 broadcast_in_dim.23
  83.4 10.0 %all-to-all-start.2 = ((f32[32,1,1280]{2,1,0:T(1,128)}), f32[32,1,1280]{2,1,0:T(1,128)S(1)}, u32[]{:S(2)}, u32[]{:S(2)}) async-start(f32[32,1,1280]{2,1,0:T(1,128)} %broadcast_in_dim.23), calls=%async_computation.2 | async-start | bytes 327680 | tf_op jit(solution)/shard_map/all_to_all | solution.py:333
  93.4 1.2 %unpack.1 = bf16[64,3840]{1,0:T(8,128)(2,1)} custom-call(bf16[16,128,128]{2,1,0:T(8,128)(2,1)S(1)} %all-to-all-done.1.in_ref), custom_call_target="tpu_custom_call" | custom-call | flops 1000000000 | bytes 1048576 | tf_op jit(solution)/shard_map/unpack/pallas_call | solution.py:226
  94.6 1.8 %all-to-all-done.2 = f32[32,1,1280]{2,1,0:T(1,128)S(1)} async-done(((f32[32,1,1280]{2,1,0:T(1,128)}), f32[32,1,1280]{2,1,0:T(1,128)S(1)}, u32[]{:S(2)}, u32[]{:S(2)}) %all-to-all-start.2) | async-done | bytes 163872 | tf_op jit(solution)/shard_map/all_to_all | solution.py:333
  96.5 0.7 reduce_sum.19
  (10 shorter events, 0.1 us)
Async XLA Ops:
  11.2 9.3 %collective-permute-start = (f32[1,640]{1,0:T(1,128)}, f32[1,640]{1,0:T(1,128)S(1)}, u32[]{:S(2)}, u32[]{:S(2)}) collective-permute-start(f32[1,640]{1,0:T(1,128)} %get-tuple-element.13.given_before), channel_id=1, source_target_pairs={{16,336},{48,368},{80,272},{112,304},{144,464},{176,496},{208,400}... | collective-permute-start | bytes 7688 | tf_op jit(solution)/shard_map/ppermute | solution.py:245
  20.4 32.7 %all-to-all-start = ((bf16[16,160,128]{2,1,0:T(8,128)(2,1)}), bf16[16,160,128]{2,1,0:T(8,128)(2,1)S(1)}, u32[]{:S(2)}, u32[]{:S(2)}) async-start(bf16[16,160,128]{2,1,0:T(8,128)(2,1)} %get-tuple-element.14), calls=%async_computation | async-start | bytes 1310720 | tf_op jit(solution)/shard_map/all_to_all | solution.py:292
  37.3 0.8 collective-permute-start.1
  38.0 0.7 copy-start
  38.8 4.3 %collective-permute-start.2 = (f32[320]{0:T(512)S(1)}, f32[320]{0:T(512)S(1)}, u32[]{:S(2)}, u32[]{:S(2)}) collective-permute-start(f32[320]{0:T(512)S(1)} %get-tuple-element.21), channel_id=1, source_target_pairs={{0,64},{16,48},{32,96},{48,16},{64,0},{80,112},{96,32},{112,80},{1... | collective-permute-start | bytes 3848 | tf_op jit(solution)/shard_map/ppermute | solution.py:245
  58.1 24.3 %all-to-all-start.1 = ((bf16[16,128,128]{2,1,0:T(8,128)(2,1)}), bf16[16,128,128]{2,1,0:T(8,128)(2,1)S(1)}, u32[]{:S(2)}, u32[]{:S(2)}) async-start(bf16[16,128,128]{2,1,0:T(8,128)(2,1)} %big.1), calls=%async_computation.1 | async-start | bytes 1048576 | tf_op jit(solution)/shard_map/all_to_all | solution.py:325
  83.4 13.0 %all-to-all-start.2 = ((f32[32,1,1280]{2,1,0:T(1,128)}), f32[32,1,1280]{2,1,0:T(1,128)S(1)}, u32[]{:S(2)}, u32[]{:S(2)}) async-start(f32[32,1,1280]{2,1,0:T(1,128)} %broadcast_in_dim.23), calls=%async_computation.2 | async-start | bytes 327680 | tf_op jit(solution)/shard_map/all_to_all | solution.py:333

commit v6 on v5

--- a/solution.py
+++ b/solution.py
@@ -17,7 +17,7 @@
 IN_ROWS = 2 * HEAD
 OUT_ROWS = 3 * HEAD // 2
 SUM_ROWS = 8
-STEPS = (((2, 2), (4, 4)), ((20, 4), (2, 2)))
+STEPS = (((2, 2), (8, 8)), ((20, 4), (2, 2)))
 SHARE = HEADS * HEAD // 4
 EXPONENT = SCALE * math.log2(math.e)
 F32 = jnp.float32
@@ -213,6 +213,21 @@
         out_ref[2 * pair + 1] = jnp.concatenate([two, extra], axis=0).astype(BF16)
 
 
+def spread_kernel(in_ref, out_ref):
+    image = lax.axis_index("dp")
+    quarters = [image // first % 2 * 2 + image // second % 2 for (_, first), (_, second) in STEPS]
+    quarter = jnp.where(image % 2 == 0, *quarters)
+    sums = in_ref[:, OUT_ROWS:].astype(F32)
+    sums = sums[:, : SUM_ROWS // 2] + sums[:, SUM_ROWS // 2 :]
+    share = jnp.sum(sums[:, :3], axis=0)
+    share = jnp.concatenate([share[at : at + 1] for at in range(3)], axis=1)[:, :SHARE]
+    columns = lax.broadcasted_iota(jnp.int32, (1, HEADS * HEAD), 1) - quarter * SHARE
+    share = jnp.concatenate([share] * 4, axis=1)
+    big = jnp.concatenate([sums[head, 3:, :HEAD] for head in range(HEADS)], axis=1)
+    total = big + jnp.where((columns >= 0) & (columns < SHARE), share, 0.0)
+    out_ref[...] = jnp.broadcast_to(total[None], out_ref.shape)
+
+
 def unpack_kernel(in_ref, out_ref):
     half = LANES // 2
     parts = []
@@ -324,15 +339,16 @@
     )
     home = lax.all_to_all(back, "seq", 0, 0, axis_index_groups=ring, tiled=True)
 
-    extra = home[:, OUT_ROWS:].astype(F32)
-    extra = extra[:, :4] + extra[:, 4:]
-    share = jnp.sum(extra[:, :3], axis=0).reshape(3 * LANES)[:SHARE]
-    quarters = [image // first % 2 * 2 + image // second % 2 for (_, first), (_, second) in STEPS]
-    held = jnp.arange(4) == jnp.where(image % 2 == 0, *quarters)
-    total = extra[:, 3, :HEAD].reshape(HEADS * HEAD) + jnp.where(held[:, None], share, 0.0).reshape(HEADS * HEAD)
-    everyone = lax.all_to_all(
-        jnp.broadcast_to(total, (images, 1, HEADS * HEAD)), "dp", 0, 0, axis_index_groups=plane, tiled=True
-    )
+    total = call(
+        spread_kernel,
+        jax.ShapeDtypeStruct((images, 1, HEADS * HEAD), F32),
+        [VMEM],
+        VMEM,
+        (home,),
+        mebibytes=8,
+        name="spread",
+    )
+    everyone = lax.all_to_all(total, "dp", 0, 0, axis_index_groups=plane, tiled=True)
     bias_grad = jnp.sum(everyone, axis=(0, 1))
 
     big_out = call(

time: 97.7 us -> 96.3 us (0.986)
  blocking collectives: 0 us -> 25.1 us
  waiting for transfers between devices: 27.4 us -> 14.2 us
  starting transfers between devices: 49.7 us -> 37.6 us
    all_to_all x0 -> x1, blocking collectives: none -> 25.1 us  [local(): home = lax.all_to_all(back, 'seq', 0, 0, axis_index_groups=ring, tiled=True)]
    all_to_all x2 -> x1, waiting for transfers between devices: 15.1 us -> 1.83 us  [local(): lax.all_to_all(total, 'dp', 0, 0, axis_index_groups=plane, tiled=True)]
    all_to_all x2 -> x1, starting transfers between devices: 21 us -> 8.98 us  [local(): lax.all_to_all(total, 'dp', 0, 0, axis_index_groups=plane, tiled=True)]
    pallas_call x4 -> x5, Pallas kernels: 16.7 us -> 16.7 us  [call(): pl.pallas_call(kernel, out_shape=shapes, in_specs=in_specs, out_specs=out...]
  transfers between devices with their start and end apart: 6 -> 5, of which waited for: 5 -> 4; matrix products, arithmetic and copies ran while one was open for 0% -> 0% of each run, Pallas kernels for 1% -> 1%
where the time goes in v6:
time: 96.3 us; the launch traced here: 95.9 us
  starting transfers between devices  37.6 us (39%)
  blocking collectives  25.1 us (26%)
  Pallas kernels  16.7 us (17%)
  waiting for transfers between devices  14.2 us (15%)
    all_to_all x1, blocking collectives, local(): home = lax.all_to_all(back, 'seq', 0, 0, axis_index_groups=ring, tiled=True)  25.1 us
    all_to_all x1, starting transfers between devices, local(): got = lax.all_to_all(sent, 'seq', 0, 0, axis_index_groups=ring, tiled=True)  16.8 us
    pallas_call x5, Pallas kernels, call(): pl.pallas_call(kernel, out_shape=shapes, in_specs=in_specs, out_specs=out...  16.7 us
    ppermute x3, starting transfers between devices, halved(): return lax.ppermute(given, 'dp', pairs)  11.9 us
    all_to_all x1, waiting for transfers between devices, local(): got = lax.all_to_all(sent, 'seq', 0, 0, axis_index_groups=ring, tiled=True)  9.97 us
    all_to_all x1, starting transfers between devices, local(): lax.all_to_all(total, 'dp', 0, 0, axis_index_groups=plane, tiled=True)  8.98 us
    ppermute x3, waiting for transfers between devices, halved(): return lax.ppermute(given, 'dp', pairs)  2.39 us
  transfers between devices with their start and end apart: 5, of which 4 were waited for; matrix products, arithmetic and copies ran while one was open for 0% of the time, Pallas kernels for 1%

profile of v6, /device:TPU:1, one launch (start us, length us, event | category | flops | bytes accessed | tf_op | source)
XLA Modules:
  0.0 95.9 jit_solution(11980920457243415043)
XLA Ops:
  0.6 10.5 %pack.1 = (bf16[16,160,128]{2,1,0:T(8,128)(2,1)}, bf16[128,3840]{1,0:T(8,128)(2,1)}, f32[1,640]{1,0:T(1,128)}, f32[1,640]{1,0:T(1,128)}) custom-call(bf16[64,3840]{1,0:T(8,128)(2,1)} %qkv_hbm.1, bf16[64,1280]{1,0:T(8,128)(2,1)} %grad_hbm.1, bf16[128,3840]{1,0:T(8,128)(2,1)} %small_qkv.3, bf16[128,1280]{1,0:T(8,128)(2,1)} %small_grad.3, s32[1,128]{1,0:T(1,128)} %ids_hbm.3), custom_call_target="tpu_custom_call" | custom-call | bytes 1048576 | tf_op jit(solution)/shard_map/pack/pallas_call | solution.py:241
  11.2 8.1 %collective-permute-start = (f32[1,640]{1,0:T(1,128)}, f32[1,640]{1,0:T(1,128)S(1)}, u32[]{:S(2)}, u32[]{:S(2)}) collective-permute-start(f32[1,640]{1,0:T(1,128)} %get-tuple-element.13.given_before), channel_id=1, source_target_pairs={{16,336},{48,368},{80,272},{112,304},{144,464},{176,496},{208,400}... | collective-permute-start | bytes 7688 | tf_op jit(solution)/shard_map/ppermute | solution.py:260
  19.3 1.2 %collective-permute-done = f32[1,640]{1,0:T(1,128)S(1)} collective-permute-done((f32[1,640]{1,0:T(1,128)}, f32[1,640]{1,0:T(1,128)S(1)}, u32[]{:S(2)}, u32[]{:S(2)}) %collective-permute-start) | collective-permute-done | bytes 2592 | tf_op jit(solution)/shard_map/ppermute | solution.py:260
  20.4 16.8 %all-to-all-start = ((bf16[16,160,128]{2,1,0:T(8,128)(2,1)}), bf16[16,160,128]{2,1,0:T(8,128)(2,1)S(1)}, u32[]{:S(2)}, u32[]{:S(2)}) async-start(bf16[16,160,128]{2,1,0:T(8,128)(2,1)} %get-tuple-element.14), calls=%async_computation | async-start | bytes 1310720 | tf_op jit(solution)/shard_map/all_to_all | solution.py:307
  37.3 0.7 collective-permute-start.1
  38.0 0.0 copy-start
  38.0 0.0 collective-permute-done.1
  38.0 0.7 copy-done
  38.7 0.1 dynamic-slice_reduce_fusion
  38.8 3.1 %collective-permute-start.2 = (f32[320]{0:T(512)S(1)}, f32[320]{0:T(512)S(1)}, u32[]{:S(2)}, u32[]{:S(2)}) collective-permute-start(f32[320]{0:T(512)S(1)} %get-tuple-element.21), channel_id=1, source_target_pairs={{0,128},{16,48},{32,160},{48,16},{64,192},{80,112},{96,224},{112,8... | collective-permute-start | bytes 3848 | tf_op jit(solution)/shard_map/ppermute | solution.py:260
  41.9 1.2 %collective-permute-done.2 = f32[320]{0:T(512)S(1)} collective-permute-done((f32[320]{0:T(512)S(1)}, f32[320]{0:T(512)S(1)}, u32[]{:S(2)}, u32[]{:S(2)}) %collective-permute-start.2) | collective-permute-done | bytes 1312 | tf_op jit(solution)/shard_map/ppermute | solution.py:260
  43.1 10.0 %all-to-all-done.in_ref = bf16[16,160,128]{2,1,0:T(8,128)(2,1)S(1)} async-done(((bf16[16,160,128]{2,1,0:T(8,128)(2,1)}), bf16[16,160,128]{2,1,0:T(8,128)(2,1)S(1)}, u32[]{:S(2)}, u32[]{:S(2)}) %all-to-all-start) | async-done | bytes 655392 | tf_op jit(solution)/shard_map/all_to_all | solution.py:307
  53.1 4.2 %big.1 = bf16[16,128,128]{2,1,0:T(8,128)(2,1)S(1)} custom-call(bf16[16,160,128]{2,1,0:T(8,128)(2,1)S(1)} %all-to-all-done.in_ref, f32[3,128]{1,0:T(4,128)S(1)} %pad_bitcast_fusion.sums_ref), custom_call_target="tpu_custom_call" | custom-call | flops 10000000000 | bytes 1048576 | tf_op jit(solution)/shard_map/big/pallas_call | solution.py:241
  57.3 25.1 %all_to_all.15.in_ref = bf16[16,128,128]{2,1,0:T(8,128)(2,1)S(1)} all-to-all(bf16[16,128,128]{2,1,0:T(8,128)(2,1)S(1)} %big.1), channel_id=1, replica_groups={{10,11,12,13,14,15,0,1,2,3,4,5,6,7,8,9},{26,27,28,29,30,31,16,17,18,19,..., dimensions={0} | all-to-all | bytes 1048576 | tf_op jit(solution)/shard_map/all_to_all | solution.py:340
  82.4 0.8 spread.1
  83.1 9.0 %all-to-all-start.2 = ((f32[32,1,1280]{2,1,0:T(1,128)}), f32[32,1,1280]{2,1,0:T(1,128)S(1)}, u32[]{:S(2)}, u32[]{:S(2)}) async-start(f32[32,1,1280]{2,1,0:T(1,128)} %spread.1), calls=%async_computation.2 | async-start | bytes 327680 | tf_op jit(solution)/shard_map/all_to_all | solution.py:351
  92.1 1.2 %unpack.1 = bf16[64,3840]{1,0:T(8,128)(2,1)} custom-call(bf16[16,128,128]{2,1,0:T(8,128)(2,1)S(1)} %all_to_all.15.in_ref), custom_call_target="tpu_custom_call" | custom-call | flops 1000000000 | bytes 1048576 | tf_op jit(solution)/shard_map/unpack/pallas_call | solution.py:241
  93.3 1.8 %all-to-all-done.2 = f32[32,1,1280]{2,1,0:T(1,128)S(1)} async-done(((f32[32,1,1280]{2,1,0:T(1,128)}), f32[32,1,1280]{2,1,0:T(1,128)S(1)}, u32[]{:S(2)}, u32[]{:S(2)}) %all-to-all-start.2) | async-done | bytes 163872 | tf_op jit(solution)/shard_map/all_to_all | solution.py:351
  95.2 0.7 reduce_sum.9
  (4 shorter events, 0.0 us)
Async XLA Ops:
  11.2 9.3 %collective-permute-start = (f32[1,640]{1,0:T(1,128)}, f32[1,640]{1,0:T(1,128)S(1)}, u32[]{:S(2)}, u32[]{:S(2)}) collective-permute-start(f32[1,640]{1,0:T(1,128)} %get-tuple-element.13.given_before), channel_id=1, source_target_pairs={{16,336},{48,368},{80,272},{112,304},{144,464},{176,496},{208,400}... | collective-permute-start | bytes 7688 | tf_op jit(solution)/shard_map/ppermute | solution.py:260
  20.4 32.7 %all-to-all-start = ((bf16[16,160,128]{2,1,0:T(8,128)(2,1)}), bf16[16,160,128]{2,1,0:T(8,128)(2,1)S(1)}, u32[]{:S(2)}, u32[]{:S(2)}) async-start(bf16[16,160,128]{2,1,0:T(8,128)(2,1)} %get-tuple-element.14), calls=%async_computation | async-start | bytes 1310720 | tf_op jit(solution)/shard_map/all_to_all | solution.py:307
  37.3 0.8 collective-permute-start.1
  38.0 0.7 copy-start
  38.8 4.3 %collective-permute-start.2 = (f32[320]{0:T(512)S(1)}, f32[320]{0:T(512)S(1)}, u32[]{:S(2)}, u32[]{:S(2)}) collective-permute-start(f32[320]{0:T(512)S(1)} %get-tuple-element.21), channel_id=1, source_target_pairs={{0,128},{16,48},{32,160},{48,16},{64,192},{80,112},{96,224},{112,8... | collective-permute-start | bytes 3848 | tf_op jit(solution)/shard_map/ppermute | solution.py:260
  83.1 12.0 %all-to-all-start.2 = ((f32[32,1,1280]{2,1,0:T(1,128)}), f32[32,1,1280]{2,1,0:T(1,128)S(1)}, u32[]{:S(2)}, u32[]{:S(2)}) async-start(f32[32,1,1280]{2,1,0:T(1,128)} %spread.1), calls=%async_computation.2 | async-start | bytes 327680 | tf_op jit(solution)/shard_map/all_to_all | solution.py:351

commit v7 on v6

--- a/solution.py
+++ b/solution.py
@@ -302,7 +302,9 @@
         ],
         name="pack",
     )
-    late = halved(sums[1], images, 0, (1,))
+    late = lax.cond(
+        image % 2 == 1, lambda given: halved(given, images, 0, (1,)), lambda given: given, sums[1]
+    )
     sent, late = lax.optimization_barrier((sent, late))
     got = lax.all_to_all(sent, "seq", 0, 0, axis_index_groups=ring, tiled=True)
 
@@ -319,7 +321,7 @@
     )
 
     early = halved(sums[1], images, 0, (0,))
-    sums = (sums[0] + late + early).reshape(2 * SHARE)
+    sums = (sums[0] + jnp.where(image % 2 == 1, late, early)).reshape(2 * SHARE)
     upper = jnp.where(image % 2 == 0, *[image // STEPS[core][1][1] % 2 for core in range(2)])
     kept = lax.dynamic_slice(sums, (upper * SHARE,), (SHARE,))
     given = lax.dynamic_slice(sums, ((1 - upper) * SHARE,), (SHARE,))

time: 96.3 us -> 96.2 us (level)
  transfers between devices with their start and end apart: 5 -> 5, of which waited for: 4 -> 4; matrix products, arithmetic and copies ran while one was open for 0% -> 1% of each run, Pallas kernels for 1% -> 1%
where the time goes in v7:
time: 96.2 us; the launch traced here: 95.8 us
  starting transfers between devices  37.5 us (39%)
  blocking collectives  25 us (26%)
  Pallas kernels  16.7 us (17%)
  waiting for transfers between devices  13.6 us (14%)
  other arithmetic  1.38 us (1%)
    all_to_all x1, blocking collectives, local(): home = lax.all_to_all(back, 'seq', 0, 0, axis_index_groups=ring, tiled=True)  25 us
    pallas_call x5, Pallas kernels, call(): pl.pallas_call(kernel, out_shape=shapes, in_specs=in_specs, out_specs=out...  16.7 us
    all_to_all x1, starting transfers between devices, local(): got = lax.all_to_all(sent, 'seq', 0, 0, axis_index_groups=ring, tiled=True)  16.7 us
    ppermute x3, starting transfers between devices, halved(): return lax.ppermute(given, 'dp', pairs)  11.9 us
    all_to_all x1, waiting for transfers between devices, local(): got = lax.all_to_all(sent, 'seq', 0, 0, axis_index_groups=ring, tiled=True)  9.44 us
    all_to_all x1, starting transfers between devices, local(): lax.all_to_all(total, 'dp', 0, 0, axis_index_groups=plane, tiled=True)  8.98 us
    ppermute x3, waiting for transfers between devices, halved(): return lax.ppermute(given, 'dp', pairs)  2.29 us
  transfers between devices with their start and end apart: 5, of which 4 were waited for; matrix products, arithmetic and copies ran while one was open for 1% of the time, Pallas kernels for 1%

profile of v7, /device:TPU:1, one launch (start us, length us, event | category | flops | bytes accessed | tf_op | source)
XLA Modules:
  0.0 95.8 jit_solution(2730526948408442355)
XLA Ops:
  0.6 10.5 %pack.1 = (bf16[16,160,128]{2,1,0:T(8,128)(2,1)}, bf16[128,3840]{1,0:T(8,128)(2,1)}, f32[1,640]{1,0:T(1,128)}, f32[1,640]{1,0:T(1,128)S(1)}) custom-call(bf16[64,3840]{1,0:T(8,128)(2,1)} %qkv_hbm.1, bf16[64,1280]{1,0:T(8,128)(2,1)} %grad_hbm.1, bf16[128,3840]{1,0:T(8,128)(2,1)} %small_qkv.3, bf16[128,1280]{1,0:T(8,128)(2,1)} %small_grad.3, s32[1,128]{1,0:T(1,128)} %ids_hbm.3), custom_call_target="tpu_custom_call" | custom-call | bytes 1048576 | tf_op jit(solution)/shard_map/pack/pallas_call | solution.py:241
  11.2 9.2 %conditional.1 = (f32[1,640]{1,0:T(1,128)}) conditional(s32[]{:T(128)} %convert_element_type.5, f32[1,640]{1,0:T(1,128)S(1)} %get-tuple-element.18.given_before, f32[1,640]{1,0:T(1,128)S(1)} %get-tuple-element.18.given_before), branch_computations={%region_0.1_spmd, %region_1.2_spmd} | conditional | bytes 10288 | solution.py:305
  11.2 8.1 %collective-permute-start = (f32[1,640]{1,0:T(1,128)S(1)}, f32[1,640]{1,0:T(1,128)}, u32[]{:S(2)}, u32[]{:S(2)}) collective-permute-start(f32[1,640]{1,0:T(1,128)S(1)} %param.1), channel_id=1, source_target_pairs={{16,336},{48,368},{80,272},{112,304},{144,464},{176,496},{208,400}... | collective-permute-start | bytes 7688 | tf_op jit(solution)/shard_map/cond/branch_1_fun/ppermute | solution.py:260
  19.3 1.1 %collective-permute-done = f32[1,640]{1,0:T(1,128)} collective-permute-done((f32[1,640]{1,0:T(1,128)S(1)}, f32[1,640]{1,0:T(1,128)}, u32[]{:S(2)}, u32[]{:S(2)}) %collective-permute-start) | collective-permute-done | bytes 2592 | tf_op jit(solution)/shard_map/cond/branch_1_fun/ppermute | solution.py:260
  20.4 16.7 %all-to-all-start = ((bf16[16,160,128]{2,1,0:T(8,128)(2,1)}), bf16[16,160,128]{2,1,0:T(8,128)(2,1)S(1)}, u32[]{:S(2)}, u32[]{:S(2)}) async-start(bf16[16,160,128]{2,1,0:T(8,128)(2,1)} %get-tuple-element.19), calls=%async_computation | async-start | bytes 1310720 | tf_op jit(solution)/shard_map/all_to_all | solution.py:309
  37.1 0.7 collective-permute-start.1
  37.8 0.0 copy-start
  37.9 0.0 collective-permute-done.1
  37.9 0.7 copy-done
  38.5 0.7 fusion
  39.2 0.1 dynamic-slice_reduce_fusion
  39.3 3.1 %collective-permute-start.2 = (f32[320]{0:T(512)S(1)}, f32[320]{0:T(512)S(1)}, u32[]{:S(2)}, u32[]{:S(2)}) collective-permute-start(f32[320]{0:T(512)S(1)} %get-tuple-element.26), channel_id=1, source_target_pairs={{0,128},{16,48},{32,160},{48,16},{64,192},{80,112},{96,224},{112,8... | collective-permute-start | bytes 3848 | tf_op jit(solution)/shard_map/ppermute | solution.py:260
  42.4 1.2 %collective-permute-done.2 = f32[320]{0:T(512)S(1)} collective-permute-done((f32[320]{0:T(512)S(1)}, f32[320]{0:T(512)S(1)}, u32[]{:S(2)}, u32[]{:S(2)}) %collective-permute-start.2) | collective-permute-done | bytes 1312 | tf_op jit(solution)/shard_map/ppermute | solution.py:260
  43.6 9.4 %all-to-all-done.in_ref = bf16[16,160,128]{2,1,0:T(8,128)(2,1)S(1)} async-done(((bf16[16,160,128]{2,1,0:T(8,128)(2,1)}), bf16[16,160,128]{2,1,0:T(8,128)(2,1)S(1)}, u32[]{:S(2)}, u32[]{:S(2)}) %all-to-all-start) | async-done | bytes 655392 | tf_op jit(solution)/shard_map/all_to_all | solution.py:309
  53.1 4.2 %big.1 = bf16[16,128,128]{2,1,0:T(8,128)(2,1)S(1)} custom-call(bf16[16,160,128]{2,1,0:T(8,128)(2,1)S(1)} %all-to-all-done.in_ref, f32[3,128]{1,0:T(4,128)S(1)} %pad_bitcast_fusion.sums_ref), custom_call_target="tpu_custom_call" | custom-call | flops 10000000000 | bytes 1048576 | tf_op jit(solution)/shard_map/big/pallas_call | solution.py:241
  57.2 25.0 %all_to_all.15.in_ref = bf16[16,128,128]{2,1,0:T(8,128)(2,1)S(1)} all-to-all(bf16[16,128,128]{2,1,0:T(8,128)(2,1)S(1)} %big.1), channel_id=1, replica_groups={{10,11,12,13,14,15,0,1,2,3,4,5,6,7,8,9},{26,27,28,29,30,31,16,17,18,19,..., dimensions={0} | all-to-all | bytes 1048576 | tf_op jit(solution)/shard_map/all_to_all | solution.py:342
  82.2 0.8 spread.1
  83.0 9.0 %all-to-all-start.2 = ((f32[32,1,1280]{2,1,0:T(1,128)}), f32[32,1,1280]{2,1,0:T(1,128)S(1)}, u32[]{:S(2)}, u32[]{:S(2)}) async-start(f32[32,1,1280]{2,1,0:T(1,128)} %spread.1), calls=%async_computation.2 | async-start | bytes 327680 | tf_op jit(solution)/shard_map/all_to_all | solution.py:353
  92.0 1.2 %unpack.1 = bf16[64,3840]{1,0:T(8,128)(2,1)} custom-call(bf16[16,128,128]{2,1,0:T(8,128)(2,1)S(1)} %all_to_all.15.in_ref), custom_call_target="tpu_custom_call" | custom-call | flops 1000000000 | bytes 1048576 | tf_op jit(solution)/shard_map/unpack/pallas_call | solution.py:241
  93.2 1.8 %all-to-all-done.2 = f32[32,1,1280]{2,1,0:T(1,128)S(1)} async-done(((f32[32,1,1280]{2,1,0:T(1,128)}), f32[32,1,1280]{2,1,0:T(1,128)S(1)}, u32[]{:S(2)}, u32[]{:S(2)}) %all-to-all-start.2) | async-done | bytes 163872 | tf_op jit(solution)/shard_map/all_to_all | solution.py:353
  95.1 0.7 reduce_sum.9
  (3 shorter events, 0.0 us)
Async XLA Ops:
  11.2 9.2 %collective-permute-start = (f32[1,640]{1,0:T(1,128)S(1)}, f32[1,640]{1,0:T(1,128)}, u32[]{:S(2)}, u32[]{:S(2)}) collective-permute-start(f32[1,640]{1,0:T(1,128)S(1)} %param.1), channel_id=1, source_target_pairs={{16,336},{48,368},{80,272},{112,304},{144,464},{176,496},{208,400}... | collective-permute-start | bytes 7688 | tf_op jit(solution)/shard_map/cond/branch_1_fun/ppermute | solution.py:260
  20.4 32.7 %all-to-all-start = ((bf16[16,160,128]{2,1,0:T(8,128)(2,1)}), bf16[16,160,128]{2,1,0:T(8,128)(2,1)S(1)}, u32[]{:S(2)}, u32[]{:S(2)}) async-start(bf16[16,160,128]{2,1,0:T(8,128)(2,1)} %get-tuple-element.19), calls=%async_computation | async-start | bytes 1310720 | tf_op jit(solution)/shard_map/all_to_all | solution.py:309
  37.1 0.8 collective-permute-start.1
  37.8 0.7 copy-start
  39.3 4.3 %collective-permute-start.2 = (f32[320]{0:T(512)S(1)}, f32[320]{0:T(512)S(1)}, u32[]{:S(2)}, u32[]{:S(2)}) collective-permute-start(f32[320]{0:T(512)S(1)} %get-tuple-element.26), channel_id=1, source_target_pairs={{0,128},{16,48},{32,160},{48,16},{64,192},{80,112},{96,224},{112,8... | collective-permute-start | bytes 3848 | tf_op jit(solution)/shard_map/ppermute | solution.py:260
  83.0 12.0 %all-to-all-start.2 = ((f32[32,1,1280]{2,1,0:T(1,128)}), f32[32,1,1280]{2,1,0:T(1,128)S(1)}, u32[]{:S(2)}, u32[]{:S(2)}) async-start(f32[32,1,1280]{2,1,0:T(1,128)} %spread.1), calls=%async_computation.2 | async-start | bytes 327680 | tf_op jit(solution)/shard_map/all_to_all | solution.py:353

commit v8 on v7

--- a/solution.py
+++ b/solution.py
@@ -13,7 +13,7 @@
 LANES = 128
 FIRST_PART = 10
 FIRST_IMAGE = 21
-TOGETHER = 1
+PAIRS = 1
 IN_ROWS = 2 * HEAD
 OUT_ROWS = 3 * HEAD // 2
 SUM_ROWS = 8
@@ -48,7 +48,7 @@
     return [pltpu.make_async_copy(sources[at], scratch[at], sems.at[at]) for at in range(3)]
 
 
-def small_images(loads, out_hbm, kept_hbm, given_hbm, core, together, scratch):
+def small_images(loads, out_hbm, kept_hbm, given_hbm, core, pairs, scratch):
     qkv, grads, ids_ref, qkv_t, grad_t, out_t, out, query_t, kept, given, sems = scratch
     rows = qkv.shape[0]
     for load in loads:
@@ -76,13 +76,17 @@
             for which, result in enumerate((query_grad, key_grad, value_grad)):
                 out_t[place(head, which)] = result[at]
 
-    if together == HEADS:
+    if pairs == HEADS // 2:
         some(range(HEADS))
     else:
 
-        @pl.loop(0, HEADS // together)
+        @pl.loop(0, pairs)
         def _(step):
-            some([step * together + at for at in range(together)])
+            some([2 * step, 2 * step + 1])
+
+        @pl.loop(2 * pairs, HEADS)
+        def _(step):
+            some([step])
 
     sums = dot(jnp.ones((8, rows), BF16), query_t[...], 1, 1)[:1]
     half = HEADS * HEAD // 2
@@ -164,7 +168,7 @@
 
     @pl.when(late)
     def _():
-        small_images(after, small_out, kept_hbm, given_hbm, 1, TOGETHER, scratch)
+        small_images(after, small_out, kept_hbm, given_hbm, 1, PAIRS, scratch)
 
     for store in stores:
         store.wait()
@@ -178,7 +182,7 @@
         loads = small_loads(small_qkv, small_grad, ids_hbm, scratch)
         for load in loads:
             load.start()
-        small_images(loads, small_out, kept_hbm, given_hbm, 0, HEADS, scratch)
+        small_images(loads, small_out, kept_hbm, given_hbm, 0, HEADS // 2, scratch)
 
 
 def pieces(row):

time: 96.2 us -> 96 us (level)
  blocking collectives: 25 us -> 26 us
    all_to_all x1, blocking collectives: 25 us -> 26 us  [local(): home = lax.all_to_all(back, 'seq', 0, 0, axis_index_groups=ring, tiled=True)]
where the time goes in v8:
time: 96 us; the launch traced here: 95.6 us
  starting transfers between devices  37.6 us (39%)
  blocking collectives  26 us (27%)
  Pallas kernels  16 us (17%)
  waiting for transfers between devices  13.1 us (14%)
  other arithmetic  1.38 us (1%)
    all_to_all x1, blocking collectives, local(): home = lax.all_to_all(back, 'seq', 0, 0, axis_index_groups=ring, tiled=True)  26 us
    all_to_all x1, starting transfers between devices, local(): got = lax.all_to_all(sent, 'seq', 0, 0, axis_index_groups=ring, tiled=True)  16.7 us
    pallas_call x5, Pallas kernels, call(): pl.pallas_call(kernel, out_shape=shapes, in_specs=in_specs, out_specs=out...  16 us
    ppermute x3, starting transfers between devices, halved(): return lax.ppermute(given, 'dp', pairs)  11.9 us
    all_to_all x1, starting transfers between devices, local(): lax.all_to_all(total, 'dp', 0, 0, axis_index_groups=plane, tiled=True)  9 us
    all_to_all x1, waiting for transfers between devices, local(): got = lax.all_to_all(sent, 'seq', 0, 0, axis_index_groups=ring, tiled=True)  8.94 us
    ppermute x3, waiting for transfers between devices, halved(): return lax.ppermute(given, 'dp', pairs)  2.29 us
  transfers between devices with their start and end apart: 5, of which 4 were waited for; matrix products, arithmetic and copies ran while one was open for 1% of the time, Pallas kernels for 1%

profile of v8, /device:TPU:1, one launch (start us, length us, event | category | flops | bytes accessed | tf_op | source)
XLA Modules:
  0.0 95.6 jit_solution(4327557236736527426)
XLA Ops:
  0.6 9.8 %pack.1 = (bf16[16,160,128]{2,1,0:T(8,128)(2,1)}, bf16[128,3840]{1,0:T(8,128)(2,1)}, f32[1,640]{1,0:T(1,128)}, f32[1,640]{1,0:T(1,128)S(1)}) custom-call(bf16[64,3840]{1,0:T(8,128)(2,1)} %qkv_hbm.1, bf16[64,1280]{1,0:T(8,128)(2,1)} %grad_hbm.1, bf16[128,3840]{1,0:T(8,128)(2,1)} %small_qkv.3, bf16[128,1280]{1,0:T(8,128)(2,1)} %small_grad.3, s32[1,128]{1,0:T(1,128)} %ids_hbm.3), custom_call_target="tpu_custom_call" | custom-call | bytes 1048576 | tf_op jit(solution)/shard_map/pack/pallas_call | solution.py:245
  10.5 9.2 %conditional.1 = (f32[1,640]{1,0:T(1,128)}) conditional(s32[]{:T(128)} %convert_element_type.5, f32[1,640]{1,0:T(1,128)S(1)} %get-tuple-element.18.given_before, f32[1,640]{1,0:T(1,128)S(1)} %get-tuple-element.18.given_before), branch_computations={%region_0.1_spmd, %region_1.2_spmd} | conditional | bytes 10288 | solution.py:309
  10.5 8.1 %collective-permute-start = (f32[1,640]{1,0:T(1,128)S(1)}, f32[1,640]{1,0:T(1,128)}, u32[]{:S(2)}, u32[]{:S(2)}) collective-permute-start(f32[1,640]{1,0:T(1,128)S(1)} %param.1), channel_id=1, source_target_pairs={{16,336},{48,368},{80,272},{112,304},{144,464},{176,496},{208,400}... | collective-permute-start | bytes 7688 | tf_op jit(solution)/shard_map/cond/branch_1_fun/ppermute | solution.py:264
  18.6 1.1 %collective-permute-done = f32[1,640]{1,0:T(1,128)} collective-permute-done((f32[1,640]{1,0:T(1,128)S(1)}, f32[1,640]{1,0:T(1,128)}, u32[]{:S(2)}, u32[]{:S(2)}) %collective-permute-start) | collective-permute-done | bytes 2592 | tf_op jit(solution)/shard_map/cond/branch_1_fun/ppermute | solution.py:264
  19.7 16.7 %all-to-all-start = ((bf16[16,160,128]{2,1,0:T(8,128)(2,1)}), bf16[16,160,128]{2,1,0:T(8,128)(2,1)S(1)}, u32[]{:S(2)}, u32[]{:S(2)}) async-start(bf16[16,160,128]{2,1,0:T(8,128)(2,1)} %get-tuple-element.19), calls=%async_computation | async-start | bytes 1310720 | tf_op jit(solution)/shard_map/all_to_all | solution.py:313
  36.4 0.7 collective-permute-start.1
  37.1 0.0 copy-start
  37.2 0.0 collective-permute-done.1
  37.2 0.7 copy-done
  37.8 0.7 fusion
  38.5 0.1 dynamic-slice_reduce_fusion
  38.6 3.1 %collective-permute-start.2 = (f32[320]{0:T(512)S(1)}, f32[320]{0:T(512)S(1)}, u32[]{:S(2)}, u32[]{:S(2)}) collective-permute-start(f32[320]{0:T(512)S(1)} %get-tuple-element.26), channel_id=1, source_target_pairs={{0,128},{16,48},{32,160},{48,16},{64,192},{80,112},{96,224},{112,8... | collective-permute-start | bytes 3848 | tf_op jit(solution)/shard_map/ppermute | solution.py:264
  41.7 1.2 %collective-permute-done.2 = f32[320]{0:T(512)S(1)} collective-permute-done((f32[320]{0:T(512)S(1)}, f32[320]{0:T(512)S(1)}, u32[]{:S(2)}, u32[]{:S(2)}) %collective-permute-start.2) | collective-permute-done | bytes 1312 | tf_op jit(solution)/shard_map/ppermute | solution.py:264
  42.9 8.9 %all-to-all-done.in_ref = bf16[16,160,128]{2,1,0:T(8,128)(2,1)S(1)} async-done(((bf16[16,160,128]{2,1,0:T(8,128)(2,1)}), bf16[16,160,128]{2,1,0:T(8,128)(2,1)S(1)}, u32[]{:S(2)}, u32[]{:S(2)}) %all-to-all-start) | async-done | bytes 655392 | tf_op jit(solution)/shard_map/all_to_all | solution.py:313
  51.9 4.2 %big.1 = bf16[16,128,128]{2,1,0:T(8,128)(2,1)S(1)} custom-call(bf16[16,160,128]{2,1,0:T(8,128)(2,1)S(1)} %all-to-all-done.in_ref, f32[3,128]{1,0:T(4,128)S(1)} %pad_bitcast_fusion.sums_ref), custom_call_target="tpu_custom_call" | custom-call | flops 10000000000 | bytes 1048576 | tf_op jit(solution)/shard_map/big/pallas_call | solution.py:245
  56.0 26.0 %all_to_all.15.in_ref = bf16[16,128,128]{2,1,0:T(8,128)(2,1)S(1)} all-to-all(bf16[16,128,128]{2,1,0:T(8,128)(2,1)S(1)} %big.1), channel_id=1, replica_groups={{10,11,12,13,14,15,0,1,2,3,4,5,6,7,8,9},{26,27,28,29,30,31,16,17,18,19,..., dimensions={0} | all-to-all | bytes 1048576 | tf_op jit(solution)/shard_map/all_to_all | solution.py:346
  82.1 0.8 spread.1
  82.8 9.0 %all-to-all-start.2 = ((f32[32,1,1280]{2,1,0:T(1,128)}), f32[32,1,1280]{2,1,0:T(1,128)S(1)}, u32[]{:S(2)}, u32[]{:S(2)}) async-start(f32[32,1,1280]{2,1,0:T(1,128)} %spread.1), calls=%async_computation.2 | async-start | bytes 327680 | tf_op jit(solution)/shard_map/all_to_all | solution.py:357
  91.8 1.2 %unpack.1 = bf16[64,3840]{1,0:T(8,128)(2,1)} custom-call(bf16[16,128,128]{2,1,0:T(8,128)(2,1)S(1)} %all_to_all.15.in_ref), custom_call_target="tpu_custom_call" | custom-call | flops 1000000000 | bytes 1048576 | tf_op jit(solution)/shard_map/unpack/pallas_call | solution.py:245
  93.1 1.8 %all-to-all-done.2 = f32[32,1,1280]{2,1,0:T(1,128)S(1)} async-done(((f32[32,1,1280]{2,1,0:T(1,128)}), f32[32,1,1280]{2,1,0:T(1,128)S(1)}, u32[]{:S(2)}, u32[]{:S(2)}) %all-to-all-start.2) | async-done | bytes 163872 | tf_op jit(solution)/shard_map/all_to_all | solution.py:357
  94.9 0.7 reduce_sum.9
  (3 shorter events, 0.0 us)
Async XLA Ops:
  10.5 9.2 %collective-permute-start = (f32[1,640]{1,0:T(1,128)S(1)}, f32[1,640]{1,0:T(1,128)}, u32[]{:S(2)}, u32[]{:S(2)}) collective-permute-start(f32[1,640]{1,0:T(1,128)S(1)} %param.1), channel_id=1, source_target_pairs={{16,336},{48,368},{80,272},{112,304},{144,464},{176,496},{208,400}... | collective-permute-start | bytes 7688 | tf_op jit(solution)/shard_map/cond/branch_1_fun/ppermute | solution.py:264
  19.7 32.2 %all-to-all-start = ((bf16[16,160,128]{2,1,0:T(8,128)(2,1)}), bf16[16,160,128]{2,1,0:T(8,128)(2,1)S(1)}, u32[]{:S(2)}, u32[]{:S(2)}) async-start(bf16[16,160,128]{2,1,0:T(8,128)(2,1)} %get-tuple-element.19), calls=%async_computation | async-start | bytes 1310720 | tf_op jit(solution)/shard_map/all_to_all | solution.py:313
  36.4 0.8 collective-permute-start.1
  37.1 0.7 copy-start
  38.6 4.3 %collective-permute-start.2 = (f32[320]{0:T(512)S(1)}, f32[320]{0:T(512)S(1)}, u32[]{:S(2)}, u32[]{:S(2)}) collective-permute-start(f32[320]{0:T(512)S(1)} %get-tuple-element.26), channel_id=1, source_target_pairs={{0,128},{16,48},{32,160},{48,16},{64,192},{80,112},{96,224},{112,8... | collective-permute-start | bytes 3848 | tf_op jit(solution)/shard_map/ppermute | solution.py:264
  82.8 12.1 %all-to-all-start.2 = ((f32[32,1,1280]{2,1,0:T(1,128)}), f32[32,1,1280]{2,1,0:T(1,128)S(1)}, u32[]{:S(2)}, u32[]{:S(2)}) async-start(f32[32,1,1280]{2,1,0:T(1,128)} %spread.1), calls=%async_computation.2 | async-start | bytes 327680 | tf_op jit(solution)/shard_map/all_to_all | solution.py:357

commit v9 on v7

--- a/solution.py
+++ b/solution.py
@@ -315,6 +315,7 @@
         [ANY] * 3,
         (small_qkv, small_grad, small_ids, small_out, *sums),
         small_scratch,
+        mebibytes=40,
         flops=10**10,
         name="small",
         aliases={3: 0, 4: 1, 5: 2},

time: 96.2 us -> 96.4 us (level)
  no operation moved by 1% of the time
where the time goes in v9:
time: 96.4 us; the launch traced here: 96 us
  starting transfers between devices  37.8 us (39%)
  blocking collectives  25.1 us (26%)
  Pallas kernels  16.7 us (17%)
  waiting for transfers between devices  13.4 us (14%)
  other arithmetic  1.4 us (1%)
    all_to_all x1, blocking collectives, local(): home = lax.all_to_all(back, 'seq', 0, 0, axis_index_groups=ring, tiled=True)  25.1 us
    all_to_all x1, starting transfers between devices, local(): got = lax.all_to_all(sent, 'seq', 0, 0, axis_index_groups=ring, tiled=True)  16.8 us
    pallas_call x5, Pallas kernels, call(): pl.pallas_call(kernel, out_shape=shapes, in_specs=in_specs, out_specs=out...  16.7 us
    ppermute x3, starting transfers between devices, halved(): return lax.ppermute(given, 'dp', pairs)  12 us
    all_to_all x1, waiting for transfers between devices, local(): got = lax.all_to_all(sent, 'seq', 0, 0, axis_index_groups=ring, tiled=True)  9.25 us
    all_to_all x1, starting transfers between devices, local(): lax.all_to_all(total, 'dp', 0, 0, axis_index_groups=plane, tiled=True)  8.98 us
    ppermute x3, waiting for transfers between devices, halved(): return lax.ppermute(given, 'dp', pairs)  2.29 us
  transfers between devices with their start and end apart: 5, of which 4 were waited for; matrix products, arithmetic and copies ran while one was open for 1% of the time, Pallas kernels for 1%

profile of v9, /device:TPU:1, one launch (start us, length us, event | category | flops | bytes accessed | tf_op | source)
XLA Modules:
  0.0 96.0 jit_solution(18029838360687030097)
XLA Ops:
  0.6 10.5 %pack.1 = (bf16[16,160,128]{2,1,0:T(8,128)(2,1)}, bf16[128,3840]{1,0:T(8,128)(2,1)}, f32[1,640]{1,0:T(1,128)}, f32[1,640]{1,0:T(1,128)S(1)}) custom-call(bf16[64,3840]{1,0:T(8,128)(2,1)} %qkv_hbm.1, bf16[64,1280]{1,0:T(8,128)(2,1)} %grad_hbm.1, bf16[128,3840]{1,0:T(8,128)(2,1)} %small_qkv.3, bf16[128,1280]{1,0:T(8,128)(2,1)} %small_grad.3, s32[1,128]{1,0:T(1,128)} %ids_hbm.3), custom_call_target="tpu_custom_call" | custom-call | bytes 1048576 | tf_op jit(solution)/shard_map/pack/pallas_call | solution.py:241
  11.2 0.0 copy-start
  11.2 9.3 %conditional.1 = (f32[1,640]{1,0:T(1,128)}) conditional(s32[]{:T(128)} %convert_element_type.5, f32[1,640]{1,0:T(1,128)S(1)} %get-tuple-element.18.given_before, f32[1,640]{1,0:T(1,128)S(1)} %get-tuple-element.18.given_before), branch_computations={%region_0.1_spmd, %region_1.2_spmd} | conditional | bytes 10288 | solution.py:305
  11.2 8.2 %collective-permute-start = (f32[1,640]{1,0:T(1,128)S(1)}, f32[1,640]{1,0:T(1,128)}, u32[]{:S(2)}, u32[]{:S(2)}) collective-permute-start(f32[1,640]{1,0:T(1,128)S(1)} %param.1), channel_id=1, source_target_pairs={{16,336},{48,368},{80,272},{112,304},{144,464},{176,496},{208,400}... | collective-permute-start | bytes 7688 | tf_op jit(solution)/shard_map/cond/branch_1_fun/ppermute | solution.py:260
  19.5 1.1 %collective-permute-done = f32[1,640]{1,0:T(1,128)} collective-permute-done((f32[1,640]{1,0:T(1,128)S(1)}, f32[1,640]{1,0:T(1,128)}, u32[]{:S(2)}, u32[]{:S(2)}) %collective-permute-start) | collective-permute-done | bytes 2592 | tf_op jit(solution)/shard_map/cond/branch_1_fun/ppermute | solution.py:260
  20.5 16.8 %all-to-all-start = ((bf16[16,160,128]{2,1,0:T(8,128)(2,1)}), bf16[16,160,128]{2,1,0:T(8,128)(2,1)S(1)}, u32[]{:S(2)}, u32[]{:S(2)}) async-start(bf16[16,160,128]{2,1,0:T(8,128)(2,1)} %get-tuple-element.19), calls=%async_computation | async-start | bytes 1310720 | tf_op jit(solution)/shard_map/all_to_all | solution.py:309
  37.4 0.0 copy-start.3
  37.4 0.0 copy-done
  37.4 0.6 copy-done.2
  38.0 0.0 copy-done.3
  38.1 0.7 collective-permute-start.1
  38.8 0.0 collective-permute-done.1
  38.8 0.7 fusion
  39.5 0.1 dynamic-slice_reduce_fusion
  39.6 3.1 %collective-permute-start.2 = (f32[320]{0:T(512)S(1)}, f32[320]{0:T(512)S(1)}, u32[]{:S(2)}, u32[]{:S(2)}) collective-permute-start(f32[320]{0:T(512)S(1)} %get-tuple-element.26), channel_id=1, source_target_pairs={{0,128},{16,48},{32,160},{48,16},{64,192},{80,112},{96,224},{112,8... | collective-permute-start | bytes 3848 | tf_op jit(solution)/shard_map/ppermute | solution.py:260
  42.7 1.2 %collective-permute-done.2 = f32[320]{0:T(512)S(1)} collective-permute-done((f32[320]{0:T(512)S(1)}, f32[320]{0:T(512)S(1)}, u32[]{:S(2)}, u32[]{:S(2)}) %collective-permute-start.2) | collective-permute-done | bytes 1312 | tf_op jit(solution)/shard_map/ppermute | solution.py:260
  43.9 9.2 %all-to-all-done.in_ref = bf16[16,160,128]{2,1,0:T(8,128)(2,1)S(1)} async-done(((bf16[16,160,128]{2,1,0:T(8,128)(2,1)}), bf16[16,160,128]{2,1,0:T(8,128)(2,1)S(1)}, u32[]{:S(2)}, u32[]{:S(2)}) %all-to-all-start) | async-done | bytes 655392 | tf_op jit(solution)/shard_map/all_to_all | solution.py:309
  53.2 4.2 %big.1 = bf16[16,128,128]{2,1,0:T(8,128)(2,1)S(1)} custom-call(bf16[16,160,128]{2,1,0:T(8,128)(2,1)S(1)} %all-to-all-done.in_ref, f32[3,128]{1,0:T(4,128)S(1)} %pad_bitcast_fusion.sums_ref), custom_call_target="tpu_custom_call" | custom-call | flops 10000000000 | bytes 1048576 | tf_op jit(solution)/shard_map/big/pallas_call | solution.py:241
  57.4 25.1 %all_to_all.15.in_ref = bf16[16,128,128]{2,1,0:T(8,128)(2,1)S(1)} all-to-all(bf16[16,128,128]{2,1,0:T(8,128)(2,1)S(1)} %big.1), channel_id=1, replica_groups={{10,11,12,13,14,15,0,1,2,3,4,5,6,7,8,9},{26,27,28,29,30,31,16,17,18,19,..., dimensions={0} | all-to-all | bytes 1048576 | tf_op jit(solution)/shard_map/all_to_all | solution.py:343
  82.5 0.8 spread.1
  83.2 9.0 %all-to-all-start.2 = ((f32[32,1,1280]{2,1,0:T(1,128)}), f32[32,1,1280]{2,1,0:T(1,128)S(1)}, u32[]{:S(2)}, u32[]{:S(2)}) async-start(f32[32,1,1280]{2,1,0:T(1,128)} %spread.1), calls=%async_computation.2 | async-start | bytes 327680 | tf_op jit(solution)/shard_map/all_to_all | solution.py:354
  92.2 1.2 %unpack.1 = bf16[64,3840]{1,0:T(8,128)(2,1)} custom-call(bf16[16,128,128]{2,1,0:T(8,128)(2,1)S(1)} %all_to_all.15.in_ref), custom_call_target="tpu_custom_call" | custom-call | flops 1000000000 | bytes 1048576 | tf_op jit(solution)/shard_map/unpack/pallas_call | solution.py:241
  93.5 1.8 %all-to-all-done.2 = f32[32,1,1280]{2,1,0:T(1,128)S(1)} async-done(((f32[32,1,1280]{2,1,0:T(1,128)}), f32[32,1,1280]{2,1,0:T(1,128)S(1)}, u32[]{:S(2)}, u32[]{:S(2)}) %all-to-all-start.2) | async-done | bytes 163872 | tf_op jit(solution)/shard_map/all_to_all | solution.py:354
  95.3 0.7 reduce_sum.9
  (6 shorter events, 0.0 us)
Async XLA Ops:
  11.2 26.2 %copy-start = (bf16[128,3840]{1,0:T(8,128)(2,1)S(1)}, bf16[128,3840]{1,0:T(8,128)(2,1)}, u32[]{:S(2)}) copy-start(bf16[128,3840]{1,0:T(8,128)(2,1)} %small_qkv.3) | copy-start | bytes 2949124
  11.2 9.3 %collective-permute-start = (f32[1,640]{1,0:T(1,128)S(1)}, f32[1,640]{1,0:T(1,128)}, u32[]{:S(2)}, u32[]{:S(2)}) collective-permute-start(f32[1,640]{1,0:T(1,128)S(1)} %param.1), channel_id=1, source_target_pairs={{16,336},{48,368},{80,272},{112,304},{144,464},{176,496},{208,400}... | collective-permute-start | bytes 7688 | tf_op jit(solution)/shard_map/cond/branch_1_fun/ppermute | solution.py:260
  20.5 16.9 %copy-start.1 = (bf16[128,1280]{1,0:T(8,128)(2,1)S(1)}, bf16[128,1280]{1,0:T(8,128)(2,1)}, u32[]{:S(2)}) copy-start(bf16[128,1280]{1,0:T(8,128)(2,1)} %small_grad.3) | copy-start | bytes 983044
  20.5 32.7 %all-to-all-start = ((bf16[16,160,128]{2,1,0:T(8,128)(2,1)}), bf16[16,160,128]{2,1,0:T(8,128)(2,1)S(1)}, u32[]{:S(2)}, u32[]{:S(2)}) async-start(bf16[16,160,128]{2,1,0:T(8,128)(2,1)} %get-tuple-element.19), calls=%async_computation | async-start | bytes 1310720 | tf_op jit(solution)/shard_map/all_to_all | solution.py:309
  37.3 0.7 copy-start.2
  37.4 0.7 copy-start.3
  38.1 0.7 collective-permute-start.1
  39.6 4.3 %collective-permute-start.2 = (f32[320]{0:T(512)S(1)}, f32[320]{0:T(512)S(1)}, u32[]{:S(2)}, u32[]{:S(2)}) collective-permute-start(f32[320]{0:T(512)S(1)} %get-tuple-element.26), channel_id=1, source_target_pairs={{0,128},{16,48},{32,160},{48,16},{64,192},{80,112},{96,224},{112,8... | collective-permute-start | bytes 3848 | tf_op jit(solution)/shard_map/ppermute | solution.py:260
  83.2 12.0 %all-to-all-start.2 = ((f32[32,1,1280]{2,1,0:T(1,128)}), f32[32,1,1280]{2,1,0:T(1,128)S(1)}, u32[]{:S(2)}, u32[]{:S(2)}) async-start(f32[32,1,1280]{2,1,0:T(1,128)} %spread.1), calls=%async_computation.2 | async-start | bytes 327680 | tf_op jit(solution)/shard_map/all_to_all | solution.py:354
